TPU v7x, 32 devices: a whole 2x2x4 slice. The times are simulated.
32 devices in a mesh: dom: 8 (over z, y), src: 4 (over x, core).
Axes of the slice: x: 2, y: 2, z: 4, core: 2. Of those that a mesh axis runs over, the one named last changes fastest.
Arguments:
- features: bfloat16 [32768, 256], P(('dom', 'src')), may hold values from -6 to 6
- cotangent: bfloat16 [32768, 256], P(('dom', 'src')), may hold values from -6 to 6
- w_self: bfloat16 [256, 256], replicated, may hold values from -0.375 to 0.375
- w_neigh: bfloat16 [256, 256], replicated, may hold values from -0.375 to 0.375
- bias: bfloat16 [256], replicated, may hold values from -3 to 3
- send_rows: int32 [8, 4, 8, 8], P('dom', 'src'), may hold values from -1 to 1023, as said below
- edge_src: int32 [8, 4, 8192], P('dom', 'src'), may hold values from 0 to 1087, as said below
- edge_dst: int32 [8, 4, 8192], P('dom', 'src'), may hold values from 0 to 4095
- tile_count: int32 [8, 4], P('dom', 'src'), may hold values from 16 to 64, as said below
Outputs:
- activations: bfloat16 [32768, 256], P(('dom', 'src'))
- feature_grad: float32 [32768, 256], P(('dom', 'src'))
Inputs may be any that keep to these rules, and one draw needn't show every extreme that they name: `send_rows`: slots of a list are filled from the first one; some list of every owner is full; an account's own part sends it nothing. `edge_src`: every edge refers to a local row or to a filled slot. Edge slots after the first tile_count * 128 are ignored.
All inputs are finite; a program needn't handle non-finite values.
Results may differ from a plain program's by a relative error of at most 0.009.
Values may be sent and summed in bfloat16 or wider, within the bound.
A program may use at most 64 MiB of HBM per device.

v0:
```python
import jax
import jax.numpy as jnp
from jax import lax
from jax.sharding import PartitionSpec as P


def local(features, cotangent, w_self, w_neigh, bias, send_rows, edge_src, edge_dst, tile_count):
    node_rows = features.shape[0]
    feature_width = features.shape[1]
    peer_total = lax.axis_size("dom")
    senders = send_rows[0, 0]
    capacity = senders.shape[1]
    halo_total = peer_total * capacity
    sources = edge_src[0, 0]
    targets = edge_dst[0, 0]
    edge_total = sources.shape[0]
    part_total = node_rows * lax.axis_size("src")
    active = jnp.arange(edge_total) // 128 < tile_count[0, 0]
    filled = senders >= 0
    zero_half = jnp.zeros((), jnp.bfloat16)
    picked = jnp.where(filled[:, :, None], features[jnp.maximum(senders, 0)], zero_half)
    counts = jnp.zeros((part_total,), jnp.float32).at[targets].add(active.astype(jnp.float32))
    degree_all = lax.psum(counts, "src")
    inverse_all = 1.0 / jnp.maximum(degree_all, 1.0)
    inverse = lax.dynamic_slice_in_dim(inverse_all, lax.axis_index("src") * node_rows, node_rows)
    remote = lax.all_to_all(picked, "dom", split_axis=0, concat_axis=0, tiled=True).reshape(
        halo_total, feature_width
    )
    table = jnp.concatenate([features, remote], axis=0)
    taken = jnp.where(active[:, None], table[sources], zero_half)
    partial_value = (
        jnp.zeros((part_total, feature_width), jnp.float32)
        .at[targets]
        .add(taken.astype(jnp.float32))
    )
    totals = lax.psum_scatter(
        partial_value.astype(jnp.bfloat16), "src", scatter_dimension=0, tiled=True
    ).astype(jnp.float32)
    neighbour_mean = (totals * inverse[:, None]).astype(jnp.bfloat16)
    preact = (
        jnp.dot(features, w_self, preferred_element_type=jnp.float32)
        + jnp.dot(neighbour_mean, w_neigh, preferred_element_type=jnp.float32)
        + bias.astype(jnp.float32)
    )
    sigma = jax.nn.sigmoid(preact)
    outputs = (preact * sigma).astype(jnp.bfloat16)
    slope = sigma * (1.0 + preact * (1.0 - sigma))
    upstream = (cotangent.astype(jnp.float32) * slope).astype(jnp.bfloat16)
    grad_own = jnp.dot(upstream, w_self.T, preferred_element_type=jnp.float32)
    scaled = (
        jnp.dot(upstream, w_neigh.T, preferred_element_type=jnp.float32) * inverse[:, None]
    ).astype(jnp.bfloat16)
    spread = lax.all_gather(scaled, "src", axis=0, tiled=True)
    contrib = jnp.where(active[:, None], spread[targets], zero_half).astype(jnp.float32)
    grad_table = (
        jnp.zeros((node_rows + halo_total, feature_width), jnp.float32).at[sources].add(contrib)
    )
    remote_grad = grad_table[node_rows:]
    local_grad = grad_table[:node_rows]
    returned = lax.all_to_all(
        remote_grad.reshape(peer_total, capacity, feature_width).astype(jnp.bfloat16),
        "dom",
        split_axis=0,
        concat_axis=0,
        tiled=True,
    ).astype(jnp.float32)
    back_rows = jnp.where(filled, senders, node_rows)
    incoming = (
        jnp.zeros((node_rows, feature_width), jnp.float32).at[back_rows].add(returned, mode="drop")
    )
    return (outputs, grad_own + local_grad + incoming)


def solution(mesh):
    placed = (
        P(("dom", "src"), None),
        P(("dom", "src"), None),
        P(),
        P(),
        P(),
        P("dom", "src", None, None),
        P("dom", "src", None),
        P("dom", "src", None),
        P("dom", "src"),
    )
    return jax.shard_map(
        local,
        mesh=mesh,
        in_specs=placed,
        out_specs=(P(("dom", "src"), None), P(("dom", "src"), None)),
        check_vma=False,
    )
```

profile of v0, /device:TPU:0, one launch (start us, length us, event | category | flops | bytes accessed | tf_op | source)
XLA Modules:
  0.0 306.9 jit_solution(6383815861542348396)
XLA Ops:
  7.2 0.0 copy-start
  7.2 0.7 compare_select_fusion.2
  7.9 0.7 compare_bitcast_fusion
  8.6 0.1 reshape.127
  8.7 1.8 gather_fusion
  10.5 0.7 bitcast_select_fusion
  11.1 7.3 %all-to-all-start = ((bf16[8,8,256]{2,1,0:T(8,128)(2,1)}), bf16[8,8,256]{2,1,0:T(8,128)(2,1)S(1)}, u32[]{:S(2)}, u32[]{:S(2)}) async-start(bf16[8,8,256]{2,1,0:T(8,128)(2,1)} %bitcast_select_fusion), calls=%async_computation | async-start | bytes 65536 | tf_op jit(solution)/shard_map/all_to_all | solution.py:26
  18.4 0.0 reduce-scatter.2.cloned.1.call-start
  18.5 0.8 compare_select_fusion.1
  19.9 0.8 compare_select_fusion
  20.8 4.4 %all-to-all-done = bf16[8,8,256]{2,1,0:T(8,128)(2,1)S(1)} async-done(((bf16[8,8,256]{2,1,0:T(8,128)(2,1)}), bf16[8,8,256]{2,1,0:T(8,128)(2,1)S(1)}, u32[]{:S(2)}, u32[]{:S(2)}) %all-to-all-start) | async-done | bytes 32800 | tf_op jit(solution)/shard_map/all_to_all | solution.py:26
  25.1 1.1 pad_maximum_fusion
  26.2 76.8 %scatter_custom_fusion = f32[4096,256]{1,0:T(8,128)} fusion(s32[8192]{0:T(1024)S(1)} %bitcast.39, pred[8192]{0:T(1024)(128)(4,1)S(1)} %fusion.17, bf16[]{:T(256)} %constant.41.clone.1, f32[]{:T(128)} %constant.14.clone.1, bf16[1088,256]{1,0:T(8,128)(2,1)S(1)} %pad_maximum_fusion, s32[8192]{0:T(1024)S(1)} %broadcast_clamp_fusion.1), kind=kCustom, calls=%fused_computation.9 | custom fusion | flops 6291456 | bytes 4792326 | tf_op jit(solution)/shard_map/scatter-add | solution.py:34
  103.1 3.8 %convert_element_type.41 = bf16[4096,256]{1,0:T(8,128)(2,1)} convert(f32[4096,256]{1,0:T(8,128)} %scatter_custom_fusion) | non-fusion elementwise | flops 1048576 | bytes 6291456 | tf_op jit(solution)/shard_map/convert_element_type | solution.py:37
  106.9 0.0 reduce-scatter.2.cloned.1.call-update
  106.9 0.0 all-gather.2.cloned.1.call-start
  107.0 43.2 %scatter_custom_fusion.1 = f32[4096]{0:T(1024)S(1)} fusion(s32[8192]{0:T(1024)S(1)} %bitcast.40, f32[8192]{0:T(1024)S(1)} %fusion.25, f32[]{:T(128)} %constant.14.clone.1), kind=kCustom, calls=%fused_computation.50 | custom fusion | flops 8192 | bytes 16388 | tf_op jit(solution)/shard_map/scatter-add | solution.py:22
  150.2 10.3 %psum.7 = f32[4096]{0:T(1024)S(1)} all-reduce(f32[4096]{0:T(1024)S(1)} %scatter_custom_fusion.1), channel_id=1, replica_groups=mesh['dom'=8,'src'=4] {'src'}, use_global_device_ids=true, to_apply=%region_3.4 | all-reduce | flops 4096 | bytes 32768 | tf_op jit(solution)/shard_map/psum | solution.py:23
  160.5 0.3 fusion.29
  160.8 0.0 reduce-scatter.2.cloned.1.call-done
  160.9 2.6 multiply_convert_fusion
  163.4 1.1 fusion.12
  164.6 0.0 all-gather.2.cloned.1.call-update
  164.6 0.1 reshape.175
  164.7 20.0 %all-gather.2.cloned.1.call-done = bf16[4096,256]{1,0:T(8,128)(2,1)} async-done(((bf16[1024,256]{1,0:T(8,128)(2,1)}), bf16[4096,256]{1,0:T(8,128)(2,1)}) %all-gather.2.cloned.1.call-update) | async-done | bytes 2097168 | tf_op jit(solution)/shard_map/all_gather | solution.py:53
  184.7 100.2 %scatter_custom_fusion.2 = f32[1088,256]{1,0:T(8,128)S(1)} fusion(s32[8192]{0:T(1024)S(1)} %bitcast.38, pred[8192]{0:T(1024)(128)(4,1)S(1)} %fusion.17, bf16[]{:T(256)} %constant.41.clone.1, f32[]{:T(128)} %constant.14.clone.1, bf16[4096,256]{1,0:T(8,128)(2,1)} %all-gather.2.cloned.1.call-done, s32[8192]{0:T(1024)S(1)} %broadcast_clamp_fusion), kind=kCustom, calls=%fused_computation.7 | custom fusion | flops 6291456 | bytes 3252230 | tf_op jit(solution)/shard_map/scatter-add | solution.py:56
  284.9 0.6 fusion.20
  285.6 5.5 %all-to-all-start.1 = ((bf16[8,8,256]{2,1,0:T(8,128)(2,1)}), bf16[8,8,256]{2,1,0:T(8,128)(2,1)S(1)}, u32[]{:S(2)}, u32[]{:S(2)}) async-start(bf16[8,8,256]{2,1,0:T(8,128)(2,1)} %fusion.20), calls=%async_computation.2 | async-start | bytes 65536 | tf_op jit(solution)/shard_map/all_to_all | solution.py:60
  291.0 0.3 convolution_add_fusion
  291.4 6.4 %all-to-all-done.1 = bf16[8,8,256]{2,1,0:T(8,128)(2,1)S(1)} async-done(((bf16[8,8,256]{2,1,0:T(8,128)(2,1)}), bf16[8,8,256]{2,1,0:T(8,128)(2,1)S(1)}, u32[]{:S(2)}, u32[]{:S(2)}) %all-to-all-start.1) | async-done | bytes 32800 | tf_op jit(solution)/shard_map/all_to_all | solution.py:60
  297.7 1.3 scatter_custom_fusion.3
  299.1 1.0 copy-done.2
  (17 shorter events, 0.1 us)
Async XLA Ops:
  7.2 153.7 %copy-start = (bf16[256,256]{1,0:T(8,128)(2,1)S(1)}, bf16[256,256]{1,0:T(8,128)(2,1)}, u32[]{:S(2)}) copy-start(bf16[256,256]{1,0:T(8,128)(2,1)} %param.12) | copy-start | bytes 393220
  11.1 14.0 %all-to-all-start = ((bf16[8,8,256]{2,1,0:T(8,128)(2,1)}), bf16[8,8,256]{2,1,0:T(8,128)(2,1)S(1)}, u32[]{:S(2)}, u32[]{:S(2)}) async-start(bf16[8,8,256]{2,1,0:T(8,128)(2,1)} %bitcast_select_fusion), calls=%async_computation | async-start | bytes 65536 | tf_op jit(solution)/shard_map/all_to_all | solution.py:26
  18.4 142.4 %reduce-scatter.2.cloned.1.call-start = ((), (), s32[]{:S(2)}) async-start(), calls=%async_computation.3 | async-start | bytes 2621440 | tf_op jit(solution)/shard_map/reduce_scatter | solution.py:36
  103.0 47.1 %copy-start.5 = (bf16[256]{0:T(256)(128)(2,1)S(1)}, bf16[256]{0:T(256)(128)(2,1)}, u32[]{:S(2)}) copy-start(bf16[256]{0:T(256)(128)(2,1)} %param.13) | copy-start | bytes 1540
  103.0 57.5 %copy-start.1 = (bf16[1024,256]{1,0:T(8,128)(2,1)S(1)}, bf16[1024,256]{1,0:T(8,128)(2,1)}, u32[]{:S(2)}) copy-start(bf16[1024,256]{1,0:T(8,128)(2,1)} %param.9) | copy-start | bytes 1572868
  103.0 57.5 %copy-start.3 = (bf16[256,256]{1,0:T(8,128)(2,1)S(1)}, bf16[256,256]{1,0:T(8,128)(2,1)}, u32[]{:S(2)}) copy-start(bf16[256,256]{1,0:T(8,128)(2,1)} %param.11) | copy-start | bytes 393220
  103.0 57.8 %copy-start.4 = (bf16[1024,256]{1,0:T(8,128)(2,1)S(1)}, bf16[1024,256]{1,0:T(8,128)(2,1)}, u32[]{:S(2)}) copy-start(bf16[1024,256]{1,0:T(8,128)(2,1)} %param.10) | copy-start | bytes 1572868
  106.9 77.8 %all-gather.2.cloned.1.call-start = ((), (), s32[]{:S(2)}) async-start(), calls=%async_computation.4 | async-start | bytes 2621440 | tf_op jit(solution)/shard_map/all_gather | solution.py:53
  285.6 12.2 %all-to-all-start.1 = ((bf16[8,8,256]{2,1,0:T(8,128)(2,1)}), bf16[8,8,256]{2,1,0:T(8,128)(2,1)S(1)}, u32[]{:S(2)}, u32[]{:S(2)}) async-start(bf16[8,8,256]{2,1,0:T(8,128)(2,1)} %fusion.20), calls=%async_computation.2 | async-start | bytes 65536 | tf_op jit(solution)/shard_map/all_to_all | solution.py:60
  299.1 1.0 copy-start.2
Sparse Core Ops, SparseCore 0:
  107.0 28.8 reduce-scatter.1
  164.7 19.9 all-gather.1
where the time goes:
time: 308 us; the launch traced here: 307 us
  other arithmetic  230 us (75%)
  waiting for transfers between devices  30.8 us (10%)
  between operations  14.8 us (5%)
  starting transfers between devices  12.8 us (4%)
  blocking collectives  10.3 us (3%)
  matrix products  4.31 us (1%)
  local copies, waits for them, and re-layouts  3.53 us (1%)
    scatter-add x1, other arithmetic, local(): jnp.zeros((node_rows + halo_total, feature_width), jnp.float32).at[sources]  100 us
    scatter-add x1, other arithmetic, local(): partial_value = jnp.zeros((part_total, feature_width), jnp.float32).at[ta...  76.8 us
    scatter-add x1, other arithmetic, local(): jnp.zeros((part_total,), jnp.float32).at[targets]  43.2 us
    all_gather x1, waiting for transfers between devices, local(): spread = lax.all_gather(scaled, 'src', axis=0, tiled=True)  20 us
    psum x1, blocking collectives, local(): degree_all = lax.psum(counts, 'src')  10.3 us
    all_to_all x1, starting transfers between devices, local(): lax.all_to_all(picked, 'dom', split_axis=0, concat_axis=0, tiled=True)  7.28 us
    all_to_all x1, waiting for transfers between devices, local(): lax.all_to_all(remote_grad.reshape(peer_total, capacity, feature_width).a...  6.35 us
  transfers between devices with their start and end apart: 4, of which 3 were waited for; matrix products, arithmetic and copies ran while one was open for 15% of the time, Pallas kernels for 0%

commit v1 on v0

v1 whole, which is shorter than its diff:
```python
import functools

import jax
import jax.numpy as jnp
from jax import lax
from jax.experimental import pallas as pl
from jax.experimental.pallas import tpu as pltpu
from jax.sharding import PartitionSpec as P

MESH = pl.DeviceIdType.MESH
CHUNK = 256
STRIP = 64
F32 = jnp.float32
BF16 = jnp.bfloat16


def build_kernel(width, halves, word_ref, count_ref, feature_ref, sender_ref, adjacency_ref, degree_ref, picked_ref,
                 unit, stage, stage_sem, *tables):
    total_rows = tables[0].shape[0]
    lanes = len(tables)

    row_at = lax.broadcasted_iota(jnp.int32, unit.shape, 0)
    lane_at = lax.broadcasted_iota(jnp.int32, unit.shape, 1)
    unit[...] = jnp.where(
        row_at == lane_at, 1, jnp.where(row_at == lane_at + 128, 65536, 0)
    ).astype(jnp.int32)
    zeros = jnp.zeros((128, 128), jnp.int32)

    def clear(step, carry):
        for table in tables:
            table[pl.ds(pl.multiple_of(step * 128, 128), 128), :] = zeros
        return carry

    lax.fori_loop(0, total_rows // 128, clear, 0)

    def edge_tile(tile, carry):
        base = tile * 128
        for group in range(0, 128, lanes):
            words = [word_ref[base + group + k] for k in range(lanes)]
            rows = [pl.ds(lax.shift_right_logical(word, 8), 1) for word in words]
            sums = [
                tables[k][rows[k], :] + unit[pl.ds(words[k] & 255, 1), :] for k in range(lanes)
            ]
            for k in range(lanes):
                tables[k][rows[k], :] = sums[k]
        return carry

    lax.fori_loop(0, count_ref[0], edge_tile, 0)

    accounts = feature_ref.shape[0]
    slots = sender_ref.shape[1]
    chosen = lax.broadcasted_iota(jnp.int32, (accounts, slots), 0) == sender_ref[...]
    picked_ref[...] = lax.dot_general(
        chosen.astype(F32).astype(BF16), feature_ref[...], (((0,), (0,)), ((), ())), preferred_element_type=F32
    )

    degree_ref[...] = jnp.zeros_like(degree_ref)
    per_block = accounts // CHUNK
    copies = []
    for chunk in range(halves // 2):
        for side in range(2):
            first = (2 * chunk + side) * width
            columns = pl.ds(side * 128, 128)

            def unpack(step, sums, first=first, columns=columns, chunk=chunk):
                rows = pl.ds(pl.multiple_of(first + step * STRIP, STRIP), STRIP)
                packed = tables[0][rows, :]
                for table in tables[1:]:
                    packed = packed + table[rows, :]
                low = (packed & 65535).astype(F32)
                high = lax.shift_right_logical(packed, 16).astype(F32)
                out = pl.ds(pl.multiple_of(step * STRIP, STRIP), STRIP)
                stage[chunk, out, columns] = low.astype(BF16)
                stage[chunk + halves // 2, out, columns] = high.astype(BF16)
                low_sum = jnp.sum(low.reshape(STRIP // 8, 8, 128), axis=0)
                high_sum = jnp.sum(high.reshape(STRIP // 8, 8, 128), axis=0)
                return sums[0] + low_sum, sums[1] + high_sum

            start = jnp.zeros((8, 128), F32)
            low_sum, high_sum = lax.fori_loop(0, width // STRIP, unpack, (start, start))
            for at, value in ((chunk, low_sum), (chunk + halves // 2, high_sum)):
                degree_ref[at // per_block, pl.ds(at % per_block, 1), columns] = jnp.sum(
                    value, axis=0, keepdims=True
                )
        for at in (chunk, chunk + halves // 2):
            copy = pltpu.make_async_copy(stage.at[at], adjacency_ref.at[at], stage_sem.at[at])
            copy.start()
            copies.append(copy)
    for copy in copies:
        copy.wait()


def layer_kernel(doms, adjacency_ref, degree_ref, picked_ref, feature_ref, cotangent_ref, self_ref, neigh_ref,
                 bias_ref, sender_ref, act_ref, grad_ref,
                 adjacency, table_t, halo, halo_t, degree_in, inverse, own_pre,
                 foreign, kept, to_sibling, from_sibling, chip_out, chip_in, own_out, own_in, spread,
                 halo_grad, returned,
                 load_sem, halo_send, halo_recv, degree_send, degree_recv, part_send, part_recv, grad_send, grad_recv,
                 back_send, back_recv):
    part, source = lax.axis_index("dom"), lax.axis_index("src")
    chip, core = source // 2, source % 2
    sibling = chip * 2 + (1 - core)
    opposite = (1 - chip) * 2 + core
    diagonal = (1 - chip) * 2 + (1 - core)
    rows = feature_ref.shape[0]
    per_block = rows // CHUNK
    capacity = halo.shape[0] // doms

    barrier = pltpu.get_barrier_semaphore()
    for step in range(1, 4):
        pl.semaphore_signal(barrier, inc=1, device_id=(part, lax.rem(source + step, 4)), device_id_type=MESH)

    def greet(step, carry):
        pl.semaphore_signal(barrier, inc=1, device_id=(lax.rem(part + step, doms), source), device_id_type=MESH)
        return carry

    lax.fori_loop(1, doms, greet, 0)

    def load(chunk):
        return pltpu.make_async_copy(adjacency_ref.at[chunk], adjacency.at[chunk], load_sem.at[chunk])

    def load_block(block):
        def go(step, carry):
            load(block * per_block + step).start()
            return carry

        lax.fori_loop(0, per_block, go, 0)

    for block in (diagonal, opposite, sibling, source):
        load_block(block)
    table_t[...] = feature_ref[...].astype(F32).T.astype(BF16)
    pl.semaphore_wait(barrier, 3 + doms - 1)

    def slot(at):
        return pl.ds(pl.multiple_of(at * capacity, capacity), capacity)

    def halo_copy(step):
        peer = lax.rem(part + step, doms)
        return pltpu.make_async_remote_copy(
            src_ref=picked_ref.at[slot(peer)], dst_ref=halo.at[slot(part)],
            send_sem=halo_send.at[step], recv_sem=halo_recv.at[step],
            device_id=(peer, source), device_id_type=MESH)

    def back_copy(step):
        peer = lax.rem(part + step, doms)
        return pltpu.make_async_remote_copy(
            src_ref=halo_grad.at[slot(peer)], dst_ref=returned.at[slot(part)],
            send_sem=back_send.at[step], recv_sem=back_recv.at[step],
            device_id=(peer, source), device_id_type=MESH)

    def each_peer(action):
        def go(step, carry):
            action(step)
            return carry

        lax.fori_loop(1, doms, go, 0)

    each_peer(lambda step: halo_copy(step).start())

    def degree_copy(step):
        peer = lax.rem(source + step, 4)
        return pltpu.make_async_remote_copy(
            src_ref=degree_ref.at[peer], dst_ref=degree_in.at[step],
            send_sem=degree_send.at[step], recv_sem=degree_recv.at[step],
            device_id=(part, peer), device_id_type=MESH)

    for step in range(1, 4):
        degree_copy(step).start()

    def part_copy(kind, step):
        source_ref, target_ref, peer = (
            (to_sibling, from_sibling, sibling),
            (chip_out, chip_in, opposite),
            (own_out, own_in, sibling),
        )[kind]
        return pltpu.make_async_remote_copy(
            src_ref=source_ref.at[step], dst_ref=target_ref.at[step],
            send_sem=part_send.at[kind, step], recv_sem=part_recv.at[kind, step],
            device_id=(part, peer), device_id_type=MESH)

    def grad_copy(kind, step):
        owner, peer = ((source, sibling), (source, opposite), (opposite, sibling))[kind]
        at = owner * per_block + step
        return pltpu.make_async_remote_copy(
            src_ref=spread.at[at], dst_ref=spread.at[at],
            send_sem=grad_send.at[kind, step], recv_sem=grad_recv.at[kind, step],
            device_id=(part, peer), device_id_type=MESH)

    def each_chunk(action):
        def go(step, carry):
            action(step)
            return carry

        lax.fori_loop(0, per_block, go, 0)

    def from_local(at):
        return jnp.dot(table_t[...], adjacency[at, 0:rows, :], preferred_element_type=F32)

    def from_halo(at):
        return jnp.dot(halo_t[...], adjacency[at, rows:, :], preferred_element_type=F32)

    def early(step):
        at = diagonal * per_block + step
        load(at).wait()
        foreign[step] = from_local(at)

    def early_kept(step):
        at = opposite * per_block + step
        load(at).wait()
        kept[step] = from_local(at)

    each_chunk(early)
    each_chunk(early_kept)
    halo[slot(part), :] = jnp.zeros((capacity, halo.shape[1]), F32)
    returned[slot(part), :] = jnp.zeros((capacity, halo.shape[1]), F32)
    each_peer(lambda step: halo_copy(step).wait_recv())
    halo_t[...] = halo[...].T.astype(BF16)

    def send_foreign(step):
        to_sibling[step] = (foreign[step] + from_halo(diagonal * per_block + step)).astype(BF16)
        part_copy(0, step).start()

    each_chunk(send_foreign)

    def send_chip(step):
        mine = kept[step] + from_halo(opposite * per_block + step)
        part_copy(0, step).wait_recv()
        chip_out[step] = (mine + from_sibling[step].astype(F32)).astype(BF16)
        part_copy(1, step).start()

    each_chunk(send_chip)

    def send_own(step):
        at = sibling * per_block + step
        load(at).wait()
        own_out[step] = (from_local(at) + from_halo(at)).astype(BF16)
        part_copy(2, step).start()

    each_chunk(send_own)

    def keep_own(step):
        at = source * per_block + step
        load(at).wait()
        foreign[step] = from_local(at) + from_halo(at)

    each_chunk(keep_own)
    own_pre[...] = jnp.dot(feature_ref[...], self_ref[...], preferred_element_type=F32) + bias_ref[...].astype(F32)

    degree = degree_ref[source]
    for step in range(1, 4):
        degree_copy(step).wait_recv()
        degree = degree + degree_in[step]
    inverse[...] = 1.0 / jnp.maximum(degree, 1.0)
    halo_grad[...] = jnp.zeros_like(halo_grad)

    def back_halo(at):
        halo_grad[...] += jnp.dot(adjacency[at, rows:, :], spread[at], preferred_element_type=F32)

    def back_local(at):
        grad_ref[...] += jnp.dot(adjacency[at, 0:rows, :], spread[at], preferred_element_type=F32)

    def dense(step):
        here = pl.ds(pl.multiple_of(step * CHUNK, CHUNK), CHUNK)
        inverse_row = inverse[pl.ds(step, 1), :]
        half = jnp.broadcast_to(inverse_row, (128, CHUNK)).T
        inverse_column = jnp.concatenate([half] * (act_ref.shape[1] // 128), axis=1)
        part_copy(2, step).wait_recv()
        part_copy(1, step).wait_recv()
        total_t = foreign[step] + own_in[step].astype(F32) + chip_in[step].astype(F32)
        mean = (total_t * inverse_row).T.astype(BF16)
        preact = own_pre[here, :] + jnp.dot(mean, neigh_ref[...], preferred_element_type=F32)
        sigma = jax.nn.sigmoid(preact)
        slope = sigma * (1.0 + preact * (1.0 - sigma))
        upstream = (cotangent_ref[here, :].astype(F32) * slope).astype(BF16)
        contract = (((1,), (1,)), ((), ()))
        at = source * per_block + step
        spread[at] = (
            lax.dot_general(upstream, neigh_ref[...], contract, preferred_element_type=F32) * inverse_column
        ).astype(BF16)
        grad_copy(1, step).start()
        grad_copy(0, step).start()
        act_ref[here, :] = (preact * sigma).astype(BF16)
        grad_ref[here, :] = lax.dot_general(upstream, self_ref[...], contract, preferred_element_type=F32)

    each_chunk(dense)

    def back_own(step):
        at = source * per_block + step
        back_halo(at)
        back_local(at)

    def back_sibling(step):
        at = sibling * per_block + step
        grad_copy(0, step).wait_recv()
        back_halo(at)
        back_local(at)

    def back_opposite(step):
        grad_copy(1, step).wait_recv()
        grad_copy(2, step).start()
        at = opposite * per_block + step
        back_halo(at)
        back_local(at)

    def back_diagonal(step):
        grad_copy(2, step).wait_recv()
        back_halo(diagonal * per_block + step)

    each_chunk(back_own)
    each_chunk(back_sibling)
    each_chunk(back_opposite)
    each_chunk(back_diagonal)
    each_peer(lambda step: back_copy(step).start())
    each_chunk(lambda step: back_local(diagonal * per_block + step))

    chosen = lax.broadcasted_iota(jnp.int32, (rows, halo.shape[0]), 0) == sender_ref[...]
    each_peer(lambda step: back_copy(step).wait_recv())
    grad_ref[...] += jnp.dot(
        chosen.astype(F32).astype(BF16), returned[...].astype(BF16), preferred_element_type=F32
    )

    each_peer(lambda step: halo_copy(step).wait_send())
    each_peer(lambda step: back_copy(step).wait_send())
    for step in range(1, 4):
        degree_copy(step).wait_send()
    for kind in range(3):
        each_chunk(lambda step, kind=kind: part_copy(kind, step).wait_send())
        each_chunk(lambda step, kind=kind: grad_copy(kind, step).wait_send())


def local(features, cotangent, w_self, w_neigh, bias, send_rows, edge_src, edge_dst, tile_count):
    rows, features_wide = features.shape
    doms, columns = lax.axis_size("dom"), lax.axis_size("src")
    slots = send_rows.shape[2] * send_rows.shape[3]
    width = rows + slots
    part_rows = rows * columns
    halves = part_rows // 256
    chunks = part_rows // CHUNK
    per_block = rows // CHUNK
    lanes = 4 if width <= 1152 else 2
    vmem = pl.BlockSpec(memory_space=pltpu.VMEM)
    smem = pl.BlockSpec(memory_space=pltpu.SMEM)
    anywhere = pl.BlockSpec(memory_space=pl.ANY)

    target = edge_dst[0, 0]
    half_rows = part_rows // 2
    upper = (target >= half_rows).astype(jnp.int32)
    within = target - upper * half_rows
    words = ((within // 128) * width + edge_src[0, 0]) * 256 + within % 128 + upper * 128
    senders = send_rows.reshape(1, slots)

    adjacency, degree, picked = pl.pallas_call(
        functools.partial(build_kernel, width, halves),
        out_shape=(
            jax.ShapeDtypeStruct((chunks, width, CHUNK), BF16),
            jax.ShapeDtypeStruct((columns, 8, CHUNK), F32),
            jax.ShapeDtypeStruct((slots, features_wide), F32),
        ),
        in_specs=[smem, smem, vmem, vmem],
        out_specs=(anywhere, vmem, vmem),
        scratch_shapes=[
            pltpu.VMEM((256, 128), jnp.int32),
            pltpu.VMEM((chunks, width, CHUNK), BF16),
            pltpu.SemaphoreType.DMA((chunks,)),
        ] + [pltpu.VMEM((halves * width, 128), jnp.int32)] * lanes,
        compiler_params=pltpu.CompilerParams(vmem_limit_bytes=58 * 1024 * 1024),
        name="count_edges",
    )(words, tile_count.reshape(1), features, senders)

    wide = features_wide
    dma = pltpu.SemaphoreType.DMA
    block_half = pltpu.VMEM((per_block, wide, CHUNK), BF16)
    block_full = pltpu.VMEM((per_block, wide, CHUNK), F32)
    return pl.pallas_call(
        functools.partial(layer_kernel, doms),
        out_shape=(
            jax.ShapeDtypeStruct((rows, wide), BF16),
            jax.ShapeDtypeStruct((rows, wide), F32),
        ),
        in_specs=[anywhere] + [vmem] * 8,
        out_specs=(vmem, vmem),
        scratch_shapes=[
            pltpu.VMEM((chunks, width, CHUNK), BF16),
            pltpu.VMEM((wide, rows), BF16),
            pltpu.VMEM((slots, wide), F32),
            pltpu.VMEM((wide, slots), BF16),
            pltpu.VMEM((4, 8, CHUNK), F32),
            pltpu.VMEM((8, CHUNK), F32),
            pltpu.VMEM((rows, wide), F32),
            block_full, block_full,
            block_half, block_half, block_half, block_half, block_half, block_half,
            pltpu.VMEM((chunks, CHUNK, wide), BF16),
            pltpu.VMEM((slots, wide), F32),
            pltpu.VMEM((slots, wide), F32),
            dma((chunks,)),
            dma((doms,)), dma((doms,)),
            dma((4,)), dma((4,)),
            dma((3, per_block)), dma((3, per_block)),
            dma((3, per_block)), dma((3, per_block)),
            dma((doms,)), dma((doms,)),
        ],
        compiler_params=pltpu.CompilerParams(
            collective_id=0, has_side_effects=True, vmem_limit_bytes=58 * 1024 * 1024
        ),
        name="layer",
    )(adjacency, degree, picked, features, cotangent, w_self, w_neigh, bias.reshape(1, wide), senders)


def solution(mesh):
    placed = (
        P(("dom", "src"), None),
        P(("dom", "src"), None),
        P(),
        P(),
        P(),
        P("dom", "src", None, None),
        P("dom", "src", None),
        P("dom", "src", None),
        P("dom", "src"),
    )
    return jax.shard_map(
        local,
        mesh=mesh,
        in_specs=placed,
        out_specs=(P(("dom", "src"), None), P(("dom", "src"), None)),
        check_vma=False,
    )
```

time: 308 us -> 78.1 us (0.25)
  other arithmetic: 230 us -> 1.43 us
  Pallas kernels: 0 us -> 67.9 us
  waiting for transfers between devices: 30.8 us -> 0 us
  between operations: 14.8 us -> 1.29 us
  starting transfers between devices: 12.8 us -> 0 us
  blocking collectives: 10.3 us -> 0 us
  matrix products: 4.31 us -> 0 us
    scatter-add x4 -> x0, other arithmetic: 222 us -> none  [the longest x1 100 us: local(): jnp.zeros((node_rows + halo_total, feature_width), jnp.float32).at[sources]]
    pallas_call x0 -> x2, Pallas kernels: none -> 67.9 us  [the longest x1 47.6 us: local(): pl.pallas_call(functools.partial(layer_kernel, doms), out_shape=(jax.Shap...]
    all_gather x1 -> x0, waiting for transfers between devices: 20 us -> none  [local(): spread = lax.all_gather(scaled, 'src', axis=0, tiled=True)]
    all_to_all x2 -> x0, starting transfers between devices: 12.8 us -> none  [the longest x1 7.28 us: local(): lax.all_to_all(picked, 'dom', split_axis=0, concat_axis=0, tiled=True)]
    all_to_all x2 -> x0, waiting for transfers between devices: 10.7 us -> none  [the longest x1 6.35 us: local(): lax.all_to_all(remote_grad.reshape(peer_total, capacity, feature_width).a...]
    psum x1 -> x0, blocking collectives: 10.3 us -> none  [local(): degree_all = lax.psum(counts, 'src')]
    dot_general x4 -> x0, matrix products: 4.31 us -> none  [the longest x1 2.57 us: local(): jnp.dot(neighbour_mean, w_neigh, preferred_element_type=jnp.float32)]
    convert_element_type x3 -> x0, other arithmetic: 3.82 us -> none  [the longest x1 3.81 us: local(): partial_value.astype(jnp.bfloat16)]
  transfers between devices with their start and end apart: 4 -> 0, of which waited for: 3 -> 0; matrix products, arithmetic and copies ran while one was open for 15% -> 0% of each run, Pallas kernels for 0% -> 0%
where the time goes in v1:
time: 78.1 us; the launch traced here: 77.2 us
  Pallas kernels  67.9 us (87%)
  local copies, waits for them, and re-layouts  6.59 us (8%)
  other arithmetic  1.43 us (2%)
  between operations  1.29 us (2%)
    pallas_call x1, Pallas kernels, local(): pl.pallas_call(functools.partial(layer_kernel, doms), out_shape=(jax.Shap...  47.6 us
    pallas_call x1, Pallas kernels, local(): pl.pallas_call(functools.partial(build_kernel, width, halves), out_shape=...  20.3 us
    unnamed x2, local copies, waits for them, and re-layouts  4.13 us

profile of v1, /device:TPU:0, one launch (start us, length us, event | category | flops | bytes accessed | tf_op | source)
XLA Modules:
  0.0 77.2 jit_solution(5761492887795825800)
XLA Ops:
  1.3 1.3 %reshape.14.sender_ref = s32[1,64]{1,0:T(1,128)} reshape(s32[1,1,8,8]{3,2,1,0:T(8,128)} %param.14) | data formatting | bytes 512 | tf_op jit(solution)/shard_map/reshape | solution.py:350
  2.6 1.2 %reshape.15.bias_ref = bf16[1,256]{1,0:T(2,128)(2,1)} reshape(bf16[256]{0:T(256)(128)(2,1)} %param.13) | data formatting | bytes 1024 | tf_op jit(solution)/shard_map/reshape | solution.py:406
  3.7 1.4 %fusion.4.word_ref = s32[8192]{0:T(1024)} fusion(s32[8192]{0:T(1024)} %bitcast.6, s32[8192]{0:T(1024)} %bitcast.7), kind=kLoop, calls=%fused_computation.9 | loop fusion | flops 229376 | bytes 98304 | tf_op jit(solution)/shard_map/add | solution.py:349
  5.2 20.3 %count_edges.1 = (bf16[16,1088,256]{2,1,0:T(8,128)(2,1)}, f32[4,8,256]{2,1,0:T(8,128)}, f32[64,256]{1,0:T(8,128)}) custom-call(s32[8192]{0:T(1024)} %fusion.4.word_ref, s32[1]{0:T(128)} %bitcast.5.count_ref, bf16[1024,256]{1,0:T(8,128)(2,1)} %feature_ref.3, s32[1,64]{1,0:T(1,128)} %reshape.14.sender_ref), custom_call_target="tpu_custom_call" | custom-call | tf_op jit(solution)/shard_map/count_edges/pallas_call | solution.py:352
  25.5 47.6 %layer.1 = (bf16[1024,256]{1,0:T(8,128)(2,1)}, f32[1024,256]{1,0:T(8,128)}) custom-call(bf16[16,1088,256]{2,1,0:T(8,128)(2,1)} %get-tuple-element.5.adjacency_ref, f32[4,8,256]{2,1,0:T(8,128)} %get-tuple-element.6.degree_ref, f32[64,256]{1,0:T(8,128)} %get-tuple-element.7.picked_ref, bf16[1024,256]{1,0:T(8,128)(2,1)} %feature_ref.3, ...), custom_call_target="tpu_custom_call" | custom-call | tf_op jit(solution)/shard_map/layer/pallas_call | solution.py:374
  73.1 1.9 %copy.14 = bf16[1024,256]{1,0:T(8,128)(2,1)} copy(bf16[1024,256]{1,0:T(8,128)(2,1)} %get-tuple-element.10) | data formatting | bytes 1048576
  74.9 2.3 %copy.15 = f32[1024,256]{1,0:T(8,128)} copy(f32[1024,256]{1,0:T(8,128)} %get-tuple-element.11) | data formatting | bytes 2097152

commit v2 on v1

--- a/solution.py
+++ b/solution.py
@@ -14,84 +14,137 @@
 BF16 = jnp.bfloat16
 
 
-def build_kernel(width, halves, word_ref, count_ref, feature_ref, sender_ref, adjacency_ref, degree_ref, picked_ref,
+def strip_of(width):
+    return max(rows for rows in range(16, 321, 16) if width % rows == 0)
+
+
+def build_kernel(width, word_ref, count_ref, feature_ref, sender_ref, adjacency_ref, degree_ref, picked_ref, row_ref,
                  unit, stage, stage_sem, *tables):
     total_rows = tables[0].shape[0]
     lanes = len(tables)
+    accounts = feature_ref.shape[0]
+    per_block = accounts // CHUNK
+    blocks = stage.shape[0] // per_block
+    strip = strip_of(width)
+    tiles = count_ref[0]
 
     row_at = lax.broadcasted_iota(jnp.int32, unit.shape, 0)
     lane_at = lax.broadcasted_iota(jnp.int32, unit.shape, 1)
-    unit[...] = jnp.where(
-        row_at == lane_at, 1, jnp.where(row_at == lane_at + 128, 65536, 0)
-    ).astype(jnp.int32)
+    unit[...] = sum(
+        jnp.where(row_at == lane_at + 128 * field, 1 << (8 * field), 0).astype(jnp.int32) for field in range(4)
+    )
     zeros = jnp.zeros((128, 128), jnp.int32)
 
-    def clear(step, carry):
-        for table in tables:
-            table[pl.ds(pl.multiple_of(step * 128, 128), 128), :] = zeros
-        return carry
-
-    lax.fori_loop(0, total_rows // 128, clear, 0)
+    def clear(chosen):
+        def go(step, carry):
+            for table in chosen:
+                table[pl.ds(pl.multiple_of(step * 128, 128), 128), :] = zeros
+            return carry
+
+        lax.fori_loop(0, total_rows // 128, go, 0)
+
+    clear(tables)
 
     def edge_tile(tile, carry):
         base = tile * 128
         for group in range(0, 128, lanes):
             words = [word_ref[base + group + k] for k in range(lanes)]
-            rows = [pl.ds(lax.shift_right_logical(word, 8), 1) for word in words]
+            rows = [pl.ds(lax.shift_right_logical(word, 9), 1) for word in words]
             sums = [
-                tables[k][rows[k], :] + unit[pl.ds(words[k] & 255, 1), :] for k in range(lanes)
+                tables[k][rows[k], :] + unit[pl.ds(words[k] & 511, 1), :] for k in range(lanes)
             ]
             for k in range(lanes):
                 tables[k][rows[k], :] = sums[k]
         return carry
 
-    lax.fori_loop(0, count_ref[0], edge_tile, 0)
-
-    accounts = feature_ref.shape[0]
-    slots = sender_ref.shape[1]
-    chosen = lax.broadcasted_iota(jnp.int32, (accounts, slots), 0) == sender_ref[...]
+    lax.fori_loop(0, tiles, edge_tile, 0)
+
+    peers, capacity = sender_ref.shape[2:]
+    slots = peers * capacity
+    sender = sender_ref[0, 0]
+    repeat = (
+        lax.broadcasted_iota(jnp.int32, (capacity, slots), 1) % capacity
+        == lax.broadcasted_iota(jnp.int32, (capacity, slots), 0)
+    ).astype(F32).astype(BF16)
+    high = jnp.dot(lax.shift_right_arithmetic(sender, 5).astype(F32).astype(BF16), repeat, preferred_element_type=F32)
+    low = jnp.dot((sender & 31).astype(F32).astype(BF16), repeat, preferred_element_type=F32)
+    mine = (
+        lax.broadcasted_iota(jnp.int32, (peers, slots), 1) // capacity
+        == lax.broadcasted_iota(jnp.int32, (peers, slots), 0)
+    )
+    row = jnp.sum(jnp.where(mine, high * 32.0 + low, 0.0), axis=0, keepdims=True).astype(jnp.int32)
+    row_ref[...] = row
+    chosen = lax.broadcasted_iota(jnp.int32, (accounts, slots), 0) == row
     picked_ref[...] = lax.dot_general(
         chosen.astype(F32).astype(BF16), feature_ref[...], (((0,), (0,)), ((), ())), preferred_element_type=F32
     )
 
     degree_ref[...] = jnp.zeros_like(degree_ref)
-    per_block = accounts // CHUNK
-    copies = []
-    for chunk in range(halves // 2):
+
+    def stage_copy(at):
+        return pltpu.make_async_copy(stage.at[at], adjacency_ref.at[at], stage_sem.at[at])
+
+    counted = jnp.zeros((8, 128), F32)
+    for piece in range(per_block):
         for side in range(2):
-            first = (2 * chunk + side) * width
+            first = (2 * piece + side) * width
             columns = pl.ds(side * 128, 128)
 
-            def unpack(step, sums, first=first, columns=columns, chunk=chunk):
-                rows = pl.ds(pl.multiple_of(first + step * STRIP, STRIP), STRIP)
+            def unpack(step, sums, first=first, columns=columns, piece=piece):
+                rows = pl.ds(pl.multiple_of(first + step * strip, 16), strip)
                 packed = tables[0][rows, :]
                 for table in tables[1:]:
                     packed = packed + table[rows, :]
-                low = (packed & 65535).astype(F32)
-                high = lax.shift_right_logical(packed, 16).astype(F32)
-                out = pl.ds(pl.multiple_of(step * STRIP, STRIP), STRIP)
-                stage[chunk, out, columns] = low.astype(BF16)
-                stage[chunk + halves // 2, out, columns] = high.astype(BF16)
-                low_sum = jnp.sum(low.reshape(STRIP // 8, 8, 128), axis=0)
-                high_sum = jnp.sum(high.reshape(STRIP // 8, 8, 128), axis=0)
-                return sums[0] + low_sum, sums[1] + high_sum
-
-            start = jnp.zeros((8, 128), F32)
-            low_sum, high_sum = lax.fori_loop(0, width // STRIP, unpack, (start, start))
-            for at, value in ((chunk, low_sum), (chunk + halves // 2, high_sum)):
-                degree_ref[at // per_block, pl.ds(at % per_block, 1), columns] = jnp.sum(
-                    value, axis=0, keepdims=True
-                )
-        for at in (chunk, chunk + halves // 2):
-            copy = pltpu.make_async_copy(stage.at[at], adjacency_ref.at[at], stage_sem.at[at])
-            copy.start()
-            copies.append(copy)
-    for copy in copies:
-        copy.wait()
+                out = pl.ds(pl.multiple_of(step * strip, 16), strip)
+                after = []
+                for field in range(4):
+                    value = packed if field == 0 else lax.shift_right_logical(packed, 8 * field)
+                    value = (value if field == 3 else value & 255).astype(F32)
+                    stage[field * per_block + piece, out, columns] = value.astype(BF16)
+                    after.append(sums[field] + jnp.sum(value.reshape(strip // 8, 8, 128), axis=0))
+                return tuple(after)
+
+            sums = lax.fori_loop(0, width // strip, unpack, (jnp.zeros((8, 128), F32),) * 4)
+            for field in range(4):
+                degree_ref[field, pl.ds(piece, 1), columns] = jnp.sum(sums[field], axis=0, keepdims=True)
+                counted = counted + sums[field]
+        for field in range(4):
+            stage_copy(field * per_block + piece).start()
+    for at in range(blocks * per_block):
+        stage_copy(at).wait()
+
+    @pl.when(jnp.sum(counted).astype(jnp.int32) != tiles * 128)
+    def _():
+        table = tables[0]
+
+        def field_pass(field, carry):
+            clear(tables[:1])
+
+            def one(edge, carry):
+                word = word_ref[edge]
+                match = jnp.where(lax.shift_right_logical(word, 7) % 4 == field, 1, 0)
+                rows = pl.ds(lax.shift_right_logical(word, 9), 1)
+                table[rows, :] = table[rows, :] + unit[pl.ds(word & 127, 1), :] * match
+                return carry
+
+            lax.fori_loop(0, tiles * 128, one, 0)
+            for piece in range(per_block):
+                for side in range(2):
+                    value = table[pl.ds((2 * piece + side) * width, width), :].astype(F32)
+                    columns = pl.ds(side * 128, 128)
+                    stage[field * per_block + piece, :, columns] = value.astype(BF16)
+                    degree_ref[field, pl.ds(piece, 1), columns] = jnp.sum(value, axis=0, keepdims=True)
+            return carry
+
+        lax.fori_loop(0, 4, field_pass, 0)
+        for at in range(blocks * per_block):
+            stage_copy(at).start()
+        for at in range(blocks * per_block):
+            stage_copy(at).wait()
 
 
 def layer_kernel(doms, adjacency_ref, degree_ref, picked_ref, feature_ref, cotangent_ref, self_ref, neigh_ref,
-                 bias_ref, sender_ref, act_ref, grad_ref,
+                 bias_ref, act_ref, grad_ref, returned_ref,
                  adjacency, table_t, halo, halo_t, degree_in, inverse, own_pre,
                  foreign, kept, to_sibling, from_sibling, chip_out, chip_in, own_out, own_in, spread,
                  halo_grad, returned,
@@ -244,7 +297,7 @@
         foreign[step] = from_local(at) + from_halo(at)
 
     each_chunk(keep_own)
-    own_pre[...] = jnp.dot(feature_ref[...], self_ref[...], preferred_element_type=F32) + bias_ref[...].astype(F32)
+    own_pre[...] = jnp.dot(feature_ref[...], self_ref[...], preferred_element_type=F32) + bias_ref[...].astype(F32).reshape(1, -1)
 
     degree = degree_ref[source]
     for step in range(1, 4):
@@ -313,12 +366,8 @@
     each_peer(lambda step: back_copy(step).start())
     each_chunk(lambda step: back_local(diagonal * per_block + step))
 
-    chosen = lax.broadcasted_iota(jnp.int32, (rows, halo.shape[0]), 0) == sender_ref[...]
     each_peer(lambda step: back_copy(step).wait_recv())
-    grad_ref[...] += jnp.dot(
-        chosen.astype(F32).astype(BF16), returned[...].astype(BF16), preferred_element_type=F32
-    )
-
+    returned_ref[...] = returned[...]
     each_peer(lambda step: halo_copy(step).wait_send())
     each_peer(lambda step: back_copy(step).wait_send())
     for step in range(1, 4):
@@ -328,57 +377,62 @@
         each_chunk(lambda step, kind=kind: grad_copy(kind, step).wait_send())
 
 
+def finish_kernel(part_act_ref, part_grad_ref, returned_ref, row_ref, act_ref, grad_ref):
+    first = pl.program_id(0) * act_ref.shape[0]
+    chosen = lax.broadcasted_iota(jnp.int32, (act_ref.shape[0], row_ref.shape[1]), 0) + first == row_ref[...]
+    act_ref[...] = part_act_ref[...]
+    grad_ref[...] = part_grad_ref[...] + jnp.dot(
+        chosen.astype(F32).astype(BF16), returned_ref[...].astype(BF16), preferred_element_type=F32
+    )
+
+
 def local(features, cotangent, w_self, w_neigh, bias, send_rows, edge_src, edge_dst, tile_count):
     rows, features_wide = features.shape
     doms, columns = lax.axis_size("dom"), lax.axis_size("src")
     slots = send_rows.shape[2] * send_rows.shape[3]
     width = rows + slots
-    part_rows = rows * columns
-    halves = part_rows // 256
-    chunks = part_rows // CHUNK
+    chunks = rows * columns // CHUNK
     per_block = rows // CHUNK
-    lanes = 4 if width <= 1152 else 2
     vmem = pl.BlockSpec(memory_space=pltpu.VMEM)
     smem = pl.BlockSpec(memory_space=pltpu.SMEM)
     anywhere = pl.BlockSpec(memory_space=pl.ANY)
 
     target = edge_dst[0, 0]
-    half_rows = part_rows // 2
-    upper = (target >= half_rows).astype(jnp.int32)
-    within = target - upper * half_rows
-    words = ((within // 128) * width + edge_src[0, 0]) * 256 + within % 128 + upper * 128
-    senders = send_rows.reshape(1, slots)
-
-    adjacency, degree, picked = pl.pallas_call(
-        functools.partial(build_kernel, width, halves),
+    within = target % rows
+    words = ((within // 128) * width + edge_src[0, 0]) * 512 + (target // rows) * 128 + within % 128
+
+    adjacency, degree, picked, row = pl.pallas_call(
+        functools.partial(build_kernel, width),
         out_shape=(
             jax.ShapeDtypeStruct((chunks, width, CHUNK), BF16),
             jax.ShapeDtypeStruct((columns, 8, CHUNK), F32),
             jax.ShapeDtypeStruct((slots, features_wide), F32),
+            jax.ShapeDtypeStruct((1, slots), jnp.int32),
         ),
         in_specs=[smem, smem, vmem, vmem],
-        out_specs=(anywhere, vmem, vmem),
+        out_specs=(anywhere, vmem, vmem, vmem),
         scratch_shapes=[
-            pltpu.VMEM((256, 128), jnp.int32),
+            pltpu.VMEM((512, 128), jnp.int32),
             pltpu.VMEM((chunks, width, CHUNK), BF16),
             pltpu.SemaphoreType.DMA((chunks,)),
-        ] + [pltpu.VMEM((halves * width, 128), jnp.int32)] * lanes,
+        ] + [pltpu.VMEM((rows // 128 * width, 128), jnp.int32)] * 4,
         compiler_params=pltpu.CompilerParams(vmem_limit_bytes=58 * 1024 * 1024),
         name="count_edges",
-    )(words, tile_count.reshape(1), features, senders)
+    )(words, tile_count.reshape(1), features, send_rows)
 
     wide = features_wide
     dma = pltpu.SemaphoreType.DMA
     block_half = pltpu.VMEM((per_block, wide, CHUNK), BF16)
     block_full = pltpu.VMEM((per_block, wide, CHUNK), F32)
-    return pl.pallas_call(
+    part_act, part_grad, returned = pl.pallas_call(
         functools.partial(layer_kernel, doms),
         out_shape=(
             jax.ShapeDtypeStruct((rows, wide), BF16),
             jax.ShapeDtypeStruct((rows, wide), F32),
+            jax.ShapeDtypeStruct((slots, wide), F32),
         ),
-        in_specs=[anywhere] + [vmem] * 8,
-        out_specs=(vmem, vmem),
+        in_specs=[anywhere] + [vmem] * 7,
+        out_specs=(vmem, vmem, vmem),
         scratch_shapes=[
             pltpu.VMEM((chunks, width, CHUNK), BF16),
             pltpu.VMEM((wide, rows), BF16),
@@ -403,7 +457,26 @@
             collective_id=0, has_side_effects=True, vmem_limit_bytes=58 * 1024 * 1024
         ),
         name="layer",
-    )(adjacency, degree, picked, features, cotangent, w_self, w_neigh, bias.reshape(1, wide), senders)
+    )(adjacency, degree, picked, features, cotangent, w_self, w_neigh, bias)
+
+    def band():
+        return pl.BlockSpec((CHUNK, wide), lambda step: (step, 0))
+
+    def whole(array):
+        return pl.BlockSpec(array.shape, lambda step: (0, 0))
+
+    return pl.pallas_call(
+        finish_kernel,
+        grid=(rows // CHUNK,),
+        out_shape=(
+            jax.ShapeDtypeStruct((rows, wide), BF16),
+            jax.ShapeDtypeStruct((rows, wide), F32),
+        ),
+        in_specs=[band(), band(), whole(returned), whole(row)],
+        out_specs=(band(), band()),
+        compiler_params=pltpu.CompilerParams(vmem_limit_bytes=32 * 1024 * 1024),
+        name="finish",
+    )(part_act, part_grad, returned, row)
 
 
 def solution(mesh):

time: 78.1 us -> 74.1 us (0.949)
  local copies, waits for them, and re-layouts: 6.59 us -> 3.1 us
    pallas_call x1 -> x2, Pallas kernels: 20.3 us -> 14.3 us  [the longest x1 12.4 us: local(): pl.pallas_call(functools.partial(build_kernel, width), out_shape=(jax.Sha...]
    pallas_call x1, Pallas kernels: 47.6 us -> 53.5 us  [local(): pl.pallas_call(functools.partial(layer_kernel, doms), out_shape=(jax.Shap...]
    reshape x2 -> x0, local copies, waits for them, and re-layouts: 2.46 us -> none  [the longest x1 1.27 us: local(): senders = send_rows.reshape(1, slots)]
    unnamed x2 -> x8, local copies, waits for them, and re-layouts: 4.13 us -> 3.1 us
where the time goes in v2:
time: 74.1 us; the launch traced here: 73.7 us
  Pallas kernels  67.8 us (91%)
  local copies, waits for them, and re-layouts  3.1 us (4%)
  other arithmetic  1.46 us (2%)
  between operations  1.32 us (2%)
    pallas_call x1, Pallas kernels, local(): pl.pallas_call(functools.partial(layer_kernel, doms), out_shape=(jax.Shap...  53.5 us
    pallas_call x1, Pallas kernels, local(): pl.pallas_call(functools.partial(build_kernel, width), out_shape=(jax.Sha...  12.4 us
    unnamed x8, local copies, waits for them, and re-layouts  3.1 us
    pallas_call x1, Pallas kernels, local(): pl.pallas_call(finish_kernel, grid=(rows // CHUNK,), out_shape=(jax.Shape...  1.92 us

profile of v2, /device:TPU:0, one launch (start us, length us, event | category | flops | bytes accessed | tf_op | source)
XLA Modules:
  0.0 73.7 jit_solution(14650291225014237854)
XLA Ops:
  1.3 1.5 %fusion.4.word_ref = s32[8192]{0:T(1024)} fusion(s32[8192]{0:T(1024)} %bitcast.4, s32[8192]{0:T(1024)} %bitcast.5), kind=kLoop, calls=%fused_computation.14 | loop fusion | flops 360448 | bytes 98304 | tf_op jit(solution)/shard_map/add | solution.py:402
  2.7 12.4 %count_edges.1 = (bf16[16,1088,256]{2,1,0:T(8,128)(2,1)}, f32[4,8,256]{2,1,0:T(8,128)}, f32[64,256]{1,0:T(8,128)}, s32[1,64]{1,0:T(1,128)}) custom-call(s32[8192]{0:T(1024)} %fusion.4.word_ref, s32[1]{0:T(128)} %bitcast.3.count_ref, bf16[1024,256]{1,0:T(8,128)(2,1)} %feature_ref.3, s32[1,1,8,8]{3,2,1,0:T(8,128)} %sender_ref.1), custom_call_target="tpu_custom_call" | custom-call | tf_op jit(solution)/shard_map/count_edges/pallas_call | solution.py:404
  15.1 0.0 copy-start.3
  15.1 53.5 %layer.1 = (bf16[1024,256]{1,0:T(8,128)(2,1)}, f32[1024,256]{1,0:T(8,128)}, f32[64,256]{1,0:T(8,128)}) custom-call(bf16[16,1088,256]{2,1,0:T(8,128)(2,1)} %get-tuple-element.9.adjacency_ref, f32[4,8,256]{2,1,0:T(8,128)} %get-tuple-element.10.degree_ref, f32[64,256]{1,0:T(8,128)} %get-tuple-element.11.picked_ref, bf16[1024,256]{1,0:T(8,128)(2,1)} %feature_ref.3, ...), custom_call_target="tpu_custom_call" | custom-call | tf_op jit(solution)/shard_map/layer/pallas_call | solution.py:427
  68.7 0.0 copy-done.3
  68.7 0.0 copy-start
  68.7 1.2 %copy-done = f32[1024,256]{1,0:T(8,128)S(1)} copy-done((f32[1024,256]{1,0:T(8,128)S(1)}, f32[1024,256]{1,0:T(8,128)}, u32[]{:S(2)}) %copy-start) | copy-done | bytes 1048600
  69.9 0.0 copy-start.1
  69.9 1.0 %copy-done.1 = bf16[1024,256]{1,0:T(8,128)(2,1)S(1)} copy-done((bf16[1024,256]{1,0:T(8,128)(2,1)S(1)}, bf16[1024,256]{1,0:T(8,128)(2,1)}, u32[]{:S(2)}) %copy-start.1) | copy-done | bytes 524312
  70.9 0.0 copy-start.2
  70.9 0.8 %copy-done.2 = f32[64,256]{1,0:T(8,128)S(1)} copy-done((f32[64,256]{1,0:T(8,128)S(1)}, f32[64,256]{1,0:T(8,128)}, u32[]{:S(2)}) %copy-start.2) | copy-done | bytes 65560
  71.8 1.9 %finish.1 = (bf16[1024,256]{1,0:T(8,128)(2,1)}, f32[1024,256]{1,0:T(8,128)}) custom-call(bf16[1024,256]{1,0:T(8,128)(2,1)S(1)} %copy-done.1, f32[1024,256]{1,0:T(8,128)S(1)} %copy-done, f32[64,256]{1,0:T(8,128)S(1)} %copy-done.2, s32[1,64]{1,0:T(1,128)S(1)} %copy-done.3), custom_call_target="tpu_custom_call" | custom-call | tf_op jit(solution)/shard_map/finish/pallas_call | solution.py:468
Async XLA Ops:
  15.1 53.5 %copy-start.3 = (s32[1,64]{1,0:T(1,128)S(1)}, s32[1,64]{1,0:T(1,128)}, u32[]{:S(2)}) copy-start(s32[1,64]{1,0:T(1,128)} %get-tuple-element.15.row_ref) | copy-start | bytes 772
  68.7 1.2 %copy-start = (f32[1024,256]{1,0:T(8,128)S(1)}, f32[1024,256]{1,0:T(8,128)}, u32[]{:S(2)}) copy-start(f32[1024,256]{1,0:T(8,128)} %get-tuple-element.13.part_grad_ref) | copy-start | bytes 3145732
  69.9 1.0 %copy-start.1 = (bf16[1024,256]{1,0:T(8,128)(2,1)S(1)}, bf16[1024,256]{1,0:T(8,128)(2,1)}, u32[]{:S(2)}) copy-start(bf16[1024,256]{1,0:T(8,128)(2,1)} %get-tuple-element.12.part_act_ref) | copy-start | bytes 1572868
  70.9 0.8 %copy-start.2 = (f32[64,256]{1,0:T(8,128)S(1)}, f32[64,256]{1,0:T(8,128)}, u32[]{:S(2)}) copy-start(f32[64,256]{1,0:T(8,128)} %get-tuple-element.14.returned_ref) | copy-start | bytes 196612

commit v3 on v2

--- a/solution.py
+++ b/solution.py
@@ -18,8 +18,16 @@
     return max(rows for rows in range(16, 321, 16) if width % rows == 0)
 
 
-def build_kernel(width, word_ref, count_ref, feature_ref, sender_ref, adjacency_ref, degree_ref, picked_ref, row_ref,
-                 unit, stage, stage_sem, *tables):
+def build_kernel(width, source_hbm, target_hbm, feature_hbm, count_ref, sender_ref,
+                 adjacency_ref, degree_ref, picked_ref, row_ref,
+                 source_ref, target_ref, feature_ref, word_vmem, word_ref, unit, stage, in_sem, stage_sem, *tables):
+    incoming = [
+        pltpu.make_async_copy(source_hbm.at[0], source_ref, in_sem.at[0]),
+        pltpu.make_async_copy(target_hbm.at[0], target_ref, in_sem.at[1]),
+        pltpu.make_async_copy(feature_hbm, feature_ref, in_sem.at[2]),
+    ]
+    for copy in incoming:
+        copy.start()
     total_rows = tables[0].shape[0]
     lanes = len(tables)
     accounts = feature_ref.shape[0]
@@ -28,6 +36,14 @@
     strip = strip_of(width)
     tiles = count_ref[0]
 
+    incoming[0].wait()
+    incoming[1].wait()
+    target = target_ref[...]
+    within = target % accounts
+    word_vmem[...] = ((within // 128) * width + source_ref[...]) * 512 + (target // accounts) * 128 + within % 128
+    word_copy = pltpu.make_async_copy(word_vmem, word_ref, in_sem.at[3])
+    word_copy.start()
+
     row_at = lax.broadcasted_iota(jnp.int32, unit.shape, 0)
     lane_at = lax.broadcasted_iota(jnp.int32, unit.shape, 1)
     unit[...] = sum(
@@ -44,11 +60,13 @@
         lax.fori_loop(0, total_rows // 128, go, 0)
 
     clear(tables)
+    word_copy.wait()
+    incoming[2].wait()
 
     def edge_tile(tile, carry):
         base = tile * 128
         for group in range(0, 128, lanes):
-            words = [word_ref[base + group + k] for k in range(lanes)]
+            words = [word_ref[0, base + group + k] for k in range(lanes)]
             rows = [pl.ds(lax.shift_right_logical(word, 9), 1) for word in words]
             sums = [
                 tables[k][rows[k], :] + unit[pl.ds(words[k] & 511, 1), :] for k in range(lanes)
@@ -121,7 +139,7 @@
             clear(tables[:1])
 
             def one(edge, carry):
-                word = word_ref[edge]
+                word = word_ref[0, edge]
                 match = jnp.where(lax.shift_right_logical(word, 7) % 4 == field, 1, 0)
                 rows = pl.ds(lax.shift_right_logical(word, 9), 1)
                 table[rows, :] = table[rows, :] + unit[pl.ds(word & 127, 1), :] * match
@@ -143,12 +161,13 @@
             stage_copy(at).wait()
 
 
-def layer_kernel(doms, adjacency_ref, degree_ref, picked_ref, feature_ref, cotangent_ref, self_ref, neigh_ref,
-                 bias_ref, act_ref, grad_ref, returned_ref,
+def layer_kernel(doms, adjacency_ref, degree_ref, picked_ref, feature_hbm, cotangent_hbm, self_hbm, neigh_hbm,
+                 bias_hbm, act_hbm, grad_hbm, returned_hbm,
+                 feature_ref, cotangent_ref, self_ref, neigh_ref, bias_ref, act_ref, grad_ref,
                  adjacency, table_t, halo, halo_t, degree_in, inverse, own_pre,
                  foreign, kept, to_sibling, from_sibling, chip_out, chip_in, own_out, own_in, spread,
                  halo_grad, returned,
-                 load_sem, halo_send, halo_recv, degree_send, degree_recv, part_send, part_recv, grad_send, grad_recv,
+                 in_sem, out_sem, load_sem, halo_send, halo_recv, degree_send, degree_recv, part_send, part_recv, grad_send, grad_recv,
                  back_send, back_recv):
     part, source = lax.axis_index("dom"), lax.axis_index("src")
     chip, core = source // 2, source % 2
@@ -179,8 +198,21 @@
 
         lax.fori_loop(0, per_block, go, 0)
 
-    for block in (diagonal, opposite, sibling, source):
-        load_block(block)
+    incoming = [
+        pltpu.make_async_copy(whole, here, in_sem.at[at])
+        for at, (whole, here) in enumerate((
+            (feature_hbm, feature_ref), (self_hbm, self_ref), (neigh_hbm, neigh_ref), (bias_hbm, bias_ref),
+            (cotangent_hbm, cotangent_ref), (degree_ref.at[source], degree_in.at[0]),
+        ))
+    ]
+    incoming[0].start()
+    load_block(diagonal)
+    load_block(opposite)
+    for copy in incoming[1:]:
+        copy.start()
+    load_block(sibling)
+    load_block(source)
+    incoming[0].wait()
     table_t[...] = feature_ref[...].astype(F32).T.astype(BF16)
     pl.semaphore_wait(barrier, 3 + doms - 1)
 
@@ -297,9 +329,11 @@
         foreign[step] = from_local(at) + from_halo(at)
 
     each_chunk(keep_own)
+    for copy in incoming[1:]:
+        copy.wait()
     own_pre[...] = jnp.dot(feature_ref[...], self_ref[...], preferred_element_type=F32) + bias_ref[...].astype(F32).reshape(1, -1)
 
-    degree = degree_ref[source]
+    degree = degree_in[0]
     for step in range(1, 4):
         degree_copy(step).wait_recv()
         degree = degree + degree_in[step]
@@ -311,6 +345,10 @@
 
     def back_local(at):
         grad_ref[...] += jnp.dot(adjacency[at, 0:rows, :], spread[at], preferred_element_type=F32)
+
+    def act_copy(step):
+        here = pl.ds(pl.multiple_of(step * CHUNK, CHUNK), CHUNK)
+        return pltpu.make_async_copy(act_ref.at[here], act_hbm.at[here], out_sem.at[step])
 
     def dense(step):
         here = pl.ds(pl.multiple_of(step * CHUNK, CHUNK), CHUNK)
@@ -333,6 +371,7 @@
         grad_copy(1, step).start()
         grad_copy(0, step).start()
         act_ref[here, :] = (preact * sigma).astype(BF16)
+        act_copy(step).start()
         grad_ref[here, :] = lax.dot_general(upstream, self_ref[...], contract, preferred_element_type=F32)
 
     each_chunk(dense)
@@ -366,15 +405,21 @@
     each_peer(lambda step: back_copy(step).start())
     each_chunk(lambda step: back_local(diagonal * per_block + step))
 
+    grad_out = pltpu.make_async_copy(grad_ref, grad_hbm, out_sem.at[per_block])
+    grad_out.start()
     each_peer(lambda step: back_copy(step).wait_recv())
-    returned_ref[...] = returned[...]
+    returned_out = pltpu.make_async_copy(returned, returned_hbm, out_sem.at[per_block + 1])
+    returned_out.start()
     each_peer(lambda step: halo_copy(step).wait_send())
     each_peer(lambda step: back_copy(step).wait_send())
     for step in range(1, 4):
         degree_copy(step).wait_send()
+    each_chunk(lambda step: act_copy(step).wait())
     for kind in range(3):
         each_chunk(lambda step, kind=kind: part_copy(kind, step).wait_send())
         each_chunk(lambda step, kind=kind: grad_copy(kind, step).wait_send())
+    grad_out.wait()
+    returned_out.wait()
 
 
 def finish_kernel(part_act_ref, part_grad_ref, returned_ref, row_ref, act_ref, grad_ref):
@@ -393,13 +438,10 @@
     width = rows + slots
     chunks = rows * columns // CHUNK
     per_block = rows // CHUNK
+    edges = edge_src.shape[2]
     vmem = pl.BlockSpec(memory_space=pltpu.VMEM)
     smem = pl.BlockSpec(memory_space=pltpu.SMEM)
     anywhere = pl.BlockSpec(memory_space=pl.ANY)
-
-    target = edge_dst[0, 0]
-    within = target % rows
-    words = ((within // 128) * width + edge_src[0, 0]) * 512 + (target // rows) * 128 + within % 128
 
     adjacency, degree, picked, row = pl.pallas_call(
         functools.partial(build_kernel, width),
@@ -409,16 +451,22 @@
             jax.ShapeDtypeStruct((slots, features_wide), F32),
             jax.ShapeDtypeStruct((1, slots), jnp.int32),
         ),
-        in_specs=[smem, smem, vmem, vmem],
+        in_specs=[anywhere, anywhere, anywhere, smem, vmem],
         out_specs=(anywhere, vmem, vmem, vmem),
         scratch_shapes=[
+            pltpu.VMEM((1, edges), jnp.int32),
+            pltpu.VMEM((1, edges), jnp.int32),
+            pltpu.VMEM((rows, features_wide), BF16),
+            pltpu.VMEM((1, edges), jnp.int32),
+            pltpu.SMEM((1, edges), jnp.int32),
             pltpu.VMEM((512, 128), jnp.int32),
             pltpu.VMEM((chunks, width, CHUNK), BF16),
+            pltpu.SemaphoreType.DMA((4,)),
             pltpu.SemaphoreType.DMA((chunks,)),
         ] + [pltpu.VMEM((rows // 128 * width, 128), jnp.int32)] * 4,
         compiler_params=pltpu.CompilerParams(vmem_limit_bytes=58 * 1024 * 1024),
         name="count_edges",
-    )(words, tile_count.reshape(1), features, send_rows)
+    )(edge_src, edge_dst, features, tile_count.reshape(1), send_rows)
 
     wide = features_wide
     dma = pltpu.SemaphoreType.DMA
@@ -431,9 +479,16 @@
             jax.ShapeDtypeStruct((rows, wide), F32),
             jax.ShapeDtypeStruct((slots, wide), F32),
         ),
-        in_specs=[anywhere] + [vmem] * 7,
-        out_specs=(vmem, vmem, vmem),
+        in_specs=[anywhere] * 8,
+        out_specs=(anywhere, anywhere, anywhere),
         scratch_shapes=[
+            pltpu.VMEM((rows, wide), BF16),
+            pltpu.VMEM((rows, wide), BF16),
+            pltpu.VMEM(w_self.shape, BF16),
+            pltpu.VMEM(w_neigh.shape, BF16),
+            pltpu.VMEM(bias.shape, BF16),
+            pltpu.VMEM((rows, wide), BF16),
+            pltpu.VMEM((rows, wide), F32),
             pltpu.VMEM((chunks, width, CHUNK), BF16),
             pltpu.VMEM((wide, rows), BF16),
             pltpu.VMEM((slots, wide), F32),
@@ -446,7 +501,7 @@
             pltpu.VMEM((chunks, CHUNK, wide), BF16),
             pltpu.VMEM((slots, wide), F32),
             pltpu.VMEM((slots, wide), F32),
-            dma((chunks,)),
+            dma((6,)), dma((per_block + 2,)), dma((chunks,)),
             dma((doms,)), dma((doms,)),
             dma((4,)), dma((4,)),
             dma((3, per_block)), dma((3, per_block)),
@@ -474,7 +529,7 @@
         ),
         in_specs=[band(), band(), whole(returned), whole(row)],
         out_specs=(band(), band()),
-        compiler_params=pltpu.CompilerParams(vmem_limit_bytes=32 * 1024 * 1024),
+        compiler_params=pltpu.CompilerParams(vmem_limit_bytes=58 * 1024 * 1024),
         name="finish",
     )(part_act, part_grad, returned, row)
 

time: 74.1 us -> 69.4 us (0.937)
  local copies, waits for them, and re-layouts: 3.1 us -> 0 us
  other arithmetic: 1.46 us -> 0 us
    pallas_call x1, Pallas kernels: 53.5 us -> 48.8 us  [local(): pl.pallas_call(functools.partial(layer_kernel, doms), out_shape=(jax.Shap...]
    unnamed x8 -> x0, local copies, waits for them, and re-layouts: 3.1 us -> none
    pallas_call x1, Pallas kernels: 12.4 us -> 14.5 us  [local(): pl.pallas_call(functools.partial(build_kernel, width), out_shape=(jax.Sha...]
    pallas_call x1, Pallas kernels: 1.92 us -> 3.83 us  [local(): pl.pallas_call(finish_kernel, grid=(rows // CHUNK,), out_shape=(jax.Shape...]
    add x1 -> x0, other arithmetic: 1.46 us -> none  [local(): (within // 128 * width + edge_src[0, 0]) * 512 + target // rows * 128]
where the time goes in v3:
time: 69.4 us; the launch traced here: 68.4 us
  Pallas kernels  67.1 us (97%)
  between operations  1.29 us (2%)
    pallas_call x1, Pallas kernels, local(): pl.pallas_call(functools.partial(layer_kernel, doms), out_shape=(jax.Shap...  48.8 us
    pallas_call x1, Pallas kernels, local(): pl.pallas_call(functools.partial(build_kernel, width), out_shape=(jax.Sha...  14.5 us
    pallas_call x1, Pallas kernels, local(): pl.pallas_call(finish_kernel, grid=(rows // CHUNK,), out_shape=(jax.Shape...  3.83 us

profile of v3, /device:TPU:0, one launch (start us, length us, event | category | flops | bytes accessed | tf_op | source)
XLA Modules:
  0.0 68.4 jit_solution(11378339650247021928)
XLA Ops:
  1.3 14.5 %count_edges.1 = (bf16[16,1088,256]{2,1,0:T(8,128)(2,1)}, f32[4,8,256]{2,1,0:T(8,128)}, f32[64,256]{1,0:T(8,128)}, s32[1,64]{1,0:T(1,128)}) custom-call(s32[1,1,8192]{2,1,0:T(1,128)} %source_hbm.1, s32[1,1,8192]{2,1,0:T(1,128)} %target_hbm.1, bf16[1024,256]{1,0:T(8,128)(2,1)} %feature_hbm.3, s32[1]{0:T(128)} %bitcast.1.count_ref, s32[1,1,8,8]{3,2,1,0:T(8,128)} %sender_ref.1), custom_call_target="tpu_custom_call" | custom-call | tf_op jit(solution)/shard_map/count_edges/pallas_call | solution.py:446
  15.8 48.8 %layer.1 = (bf16[1024,256]{1,0:T(8,128)(2,1)}, f32[1024,256]{1,0:T(8,128)}, f32[64,256]{1,0:T(8,128)}) custom-call(bf16[16,1088,256]{2,1,0:T(8,128)(2,1)} %get-tuple-element.9.adjacency_ref, f32[4,8,256]{2,1,0:T(8,128)} %get-tuple-element.10.degree_ref, f32[64,256]{1,0:T(8,128)} %get-tuple-element.11.picked_ref, bf16[1024,256]{1,0:T(8,128)(2,1)} %feature_hbm.3, ...), custom_call_target="tpu_custom_call" | custom-call | tf_op jit(solution)/shard_map/layer/pallas_call | solution.py:475
  64.6 3.8 %finish.1 = (bf16[1024,256]{1,0:T(8,128)(2,1)}, f32[1024,256]{1,0:T(8,128)}) custom-call(bf16[1024,256]{1,0:T(8,128)(2,1)} %get-tuple-element.12.part_act_ref, f32[1024,256]{1,0:T(8,128)} %get-tuple-element.13.part_grad_ref, f32[64,256]{1,0:T(8,128)} %get-tuple-element.14.returned_ref, s32[1,64]{1,0:T(1,128)} %get-tuple-element.15.row_ref), custom_call_target="tpu_custom_call" | custom-call | tf_op jit(solution)/shard_map/finish/pallas_call | solution.py:523

commit v4 on v3

--- a/solution.py
+++ b/solution.py
@@ -65,14 +65,19 @@
 
     def edge_tile(tile, carry):
         base = tile * 128
-        for group in range(0, 128, lanes):
-            words = [word_ref[0, base + group + k] for k in range(lanes)]
-            rows = [pl.ds(lax.shift_right_logical(word, 9), 1) for word in words]
-            sums = [
-                tables[k][rows[k], :] + unit[pl.ds(words[k] & 511, 1), :] for k in range(lanes)
-            ]
+        for group in range(0, 128, 2 * lanes):
+            words = [word_ref[0, base + group + k] for k in range(2 * lanes)]
+            rows = [lax.shift_right_logical(word, 9) for word in words]
+            units = [word & 511 for word in words]
+            sums = []
             for k in range(lanes):
-                tables[k][rows[k], :] = sums[k]
+                again = jnp.where(rows[k] == rows[k + lanes], units[k], 512)
+                first = unit[pl.ds(units[k], 1), :]
+                second = unit[pl.ds(units[k + lanes], 1), :] + unit[pl.ds(again, 1), :]
+                sums.append((tables[k][pl.ds(rows[k], 1), :] + first, tables[k][pl.ds(rows[k + lanes], 1), :] + second))
+            for k in range(lanes):
+                tables[k][pl.ds(rows[k], 1), :] = sums[k][0]
+                tables[k][pl.ds(rows[k + lanes], 1), :] = sums[k][1]
         return carry
 
     lax.fori_loop(0, tiles, edge_tile, 0)
@@ -313,7 +318,8 @@
         chip_out[step] = (mine + from_sibling[step].astype(F32)).astype(BF16)
         part_copy(1, step).start()
 
-    each_chunk(send_chip)
+    send_chip(0)
+    send_chip(1)
 
     def send_own(step):
         at = sibling * per_block + step
@@ -339,12 +345,24 @@
         degree = degree + degree_in[step]
     inverse[...] = 1.0 / jnp.maximum(degree, 1.0)
     halo_grad[...] = jnp.zeros_like(halo_grad)
+    grad_ref[...] = jnp.zeros_like(grad_ref)
 
     def back_halo(at):
         halo_grad[...] += jnp.dot(adjacency[at, rows:, :], spread[at], preferred_element_type=F32)
 
     def back_local(at):
         grad_ref[...] += jnp.dot(adjacency[at, 0:rows, :], spread[at], preferred_element_type=F32)
+
+    def back_own(step):
+        at = source * per_block + step
+        back_halo(at)
+        back_local(at)
+
+    def back_sibling(step):
+        at = sibling * per_block + step
+        grad_copy(0, step).wait_recv()
+        back_halo(at)
+        back_local(at)
 
     def act_copy(step):
         here = pl.ds(pl.multiple_of(step * CHUNK, CHUNK), CHUNK)
@@ -372,38 +390,35 @@
         grad_copy(0, step).start()
         act_ref[here, :] = (preact * sigma).astype(BF16)
         act_copy(step).start()
-        grad_ref[here, :] = lax.dot_general(upstream, self_ref[...], contract, preferred_element_type=F32)
-
-    each_chunk(dense)
-
-    def back_own(step):
-        at = source * per_block + step
-        back_halo(at)
-        back_local(at)
-
-    def back_sibling(step):
-        at = sibling * per_block + step
-        grad_copy(0, step).wait_recv()
-        back_halo(at)
-        back_local(at)
-
-    def back_opposite(step):
+        grad_ref[here, :] += lax.dot_general(upstream, self_ref[...], contract, preferred_element_type=F32)
+
+    for step in range(2, per_block):
+        part_copy(1, step - 2).wait_send()
+        send_chip(step)
+        dense(step - 2)
+        back_own(step - 2)
+    for step in range(per_block - 2, per_block):
+        grad_copy(1, step - 2).wait_send()
+        dense(step)
+        back_own(step)
+    for step in range(per_block):
+        back_sibling(step)
+    last = per_block - 1
+    for step in range(per_block):
         grad_copy(1, step).wait_recv()
         grad_copy(2, step).start()
-        at = opposite * per_block + step
-        back_halo(at)
-        back_local(at)
-
-    def back_diagonal(step):
-        grad_copy(2, step).wait_recv()
-        back_halo(diagonal * per_block + step)
-
-    each_chunk(back_own)
-    each_chunk(back_sibling)
-    each_chunk(back_opposite)
-    each_chunk(back_diagonal)
+        back_halo(opposite * per_block + step)
+        if step < last:
+            back_local(opposite * per_block + step)
+        if step > 0:
+            grad_copy(2, step - 1).wait_recv()
+            back_halo(diagonal * per_block + step - 1)
+            back_local(diagonal * per_block + step - 1)
+    grad_copy(2, last).wait_recv()
+    back_halo(diagonal * per_block + last)
     each_peer(lambda step: back_copy(step).start())
-    each_chunk(lambda step: back_local(diagonal * per_block + step))
+    back_local(opposite * per_block + last)
+    back_local(diagonal * per_block + last)
 
     grad_out = pltpu.make_async_copy(grad_ref, grad_hbm, out_sem.at[per_block])
     grad_out.start()
@@ -416,19 +431,41 @@
         degree_copy(step).wait_send()
     each_chunk(lambda step: act_copy(step).wait())
     for kind in range(3):
-        each_chunk(lambda step, kind=kind: part_copy(kind, step).wait_send())
-        each_chunk(lambda step, kind=kind: grad_copy(kind, step).wait_send())
+        for step in range(per_block - 2 if kind == 1 else 0, per_block):
+            part_copy(kind, step).wait_send()
+            grad_copy(kind, step).wait_send()
     grad_out.wait()
     returned_out.wait()
 
 
-def finish_kernel(part_act_ref, part_grad_ref, returned_ref, row_ref, act_ref, grad_ref):
-    first = pl.program_id(0) * act_ref.shape[0]
-    chosen = lax.broadcasted_iota(jnp.int32, (act_ref.shape[0], row_ref.shape[1]), 0) + first == row_ref[...]
-    act_ref[...] = part_act_ref[...]
-    grad_ref[...] = part_grad_ref[...] + jnp.dot(
-        chosen.astype(F32).astype(BF16), returned_ref[...].astype(BF16), preferred_element_type=F32
-    )
+def finish_kernel(part_act_ref, part_grad_ref, returned_ref, row_ref, act_ref, grad_ref, grad, returned, sem):
+    pieces = grad_ref.shape[0] // CHUNK
+
+    def piece(at):
+        return pl.ds(at * CHUNK, CHUNK)
+
+    act = pltpu.make_async_copy(part_act_ref, act_ref, sem.at[0])
+    back = pltpu.make_async_copy(returned_ref, returned, sem.at[1])
+    come = [
+        pltpu.make_async_copy(part_grad_ref.at[piece(at)], grad.at[piece(at)], sem.at[2 + at]) for at in range(pieces)
+    ]
+    back.start()
+    for copy in come:
+        copy.start()
+    act.start()
+    back.wait()
+    rows = returned[...].astype(BF16)
+    leave = []
+    for at in range(pieces):
+        chosen = lax.broadcasted_iota(jnp.int32, (CHUNK, row_ref.shape[1]), 0) + at * CHUNK == row_ref[...]
+        added = jnp.dot(chosen.astype(F32).astype(BF16), rows, preferred_element_type=F32)
+        come[at].wait()
+        grad[piece(at), :] += added
+        leave.append(pltpu.make_async_copy(grad.at[piece(at)], grad_ref.at[piece(at)], sem.at[2 + pieces + at]))
+        leave[-1].start()
+    act.wait()
+    for copy in leave:
+        copy.wait()
 
 
 def local(features, cotangent, w_self, w_neigh, bias, send_rows, edge_src, edge_dst, tile_count):
@@ -439,6 +476,7 @@
     chunks = rows * columns // CHUNK
     per_block = rows // CHUNK
     edges = edge_src.shape[2]
+    limit = (36 if width <= 1152 else 58) * 1024 * 1024
     vmem = pl.BlockSpec(memory_space=pltpu.VMEM)
     smem = pl.BlockSpec(memory_space=pltpu.SMEM)
     anywhere = pl.BlockSpec(memory_space=pl.ANY)
@@ -459,12 +497,12 @@
             pltpu.VMEM((rows, features_wide), BF16),
             pltpu.VMEM((1, edges), jnp.int32),
             pltpu.SMEM((1, edges), jnp.int32),
-            pltpu.VMEM((512, 128), jnp.int32),
+            pltpu.VMEM((520, 128), jnp.int32),
             pltpu.VMEM((chunks, width, CHUNK), BF16),
             pltpu.SemaphoreType.DMA((4,)),
             pltpu.SemaphoreType.DMA((chunks,)),
         ] + [pltpu.VMEM((rows // 128 * width, 128), jnp.int32)] * 4,
-        compiler_params=pltpu.CompilerParams(vmem_limit_bytes=58 * 1024 * 1024),
+        compiler_params=pltpu.CompilerParams(vmem_limit_bytes=limit),
         name="count_edges",
     )(edge_src, edge_dst, features, tile_count.reshape(1), send_rows)
 
@@ -509,27 +547,21 @@
             dma((doms,)), dma((doms,)),
         ],
         compiler_params=pltpu.CompilerParams(
-            collective_id=0, has_side_effects=True, vmem_limit_bytes=58 * 1024 * 1024
+            collective_id=0, has_side_effects=True, vmem_limit_bytes=limit
         ),
         name="layer",
     )(adjacency, degree, picked, features, cotangent, w_self, w_neigh, bias)
 
-    def band():
-        return pl.BlockSpec((CHUNK, wide), lambda step: (step, 0))
-
-    def whole(array):
-        return pl.BlockSpec(array.shape, lambda step: (0, 0))
-
     return pl.pallas_call(
         finish_kernel,
-        grid=(rows // CHUNK,),
         out_shape=(
             jax.ShapeDtypeStruct((rows, wide), BF16),
             jax.ShapeDtypeStruct((rows, wide), F32),
         ),
-        in_specs=[band(), band(), whole(returned), whole(row)],
-        out_specs=(band(), band()),
-        compiler_params=pltpu.CompilerParams(vmem_limit_bytes=58 * 1024 * 1024),
+        in_specs=[anywhere, anywhere, anywhere, vmem],
+        out_specs=(anywhere, anywhere),
+        scratch_shapes=[pltpu.VMEM((rows, wide), F32), pltpu.VMEM((slots, wide), F32), dma((2 + 2 * per_block,))],
+        compiler_params=pltpu.CompilerParams(vmem_limit_bytes=limit),
         name="finish",
     )(part_act, part_grad, returned, row)
 

time: 69.4 us -> 75.6 us (1.089)
  local copies, waits for them, and re-layouts: 0 us -> 6.73 us
  Pallas kernels: 67.1 us -> 66.2 us
    unnamed x0 -> x16, local copies, waits for them, and re-layouts: none -> 6.73 us
    pallas_call x1, Pallas kernels: 14.5 us -> 20 us  [local(): pl.pallas_call(functools.partial(build_kernel, width), out_shape=(jax.Sha...]
    pallas_call x1, Pallas kernels: 48.8 us -> 44.5 us  [local(): pl.pallas_call(functools.partial(layer_kernel, doms), out_shape=(jax.Shap...]
    pallas_call x1, Pallas kernels: 3.83 us -> 1.74 us  [local(): pl.pallas_call(finish_kernel, out_shape=(jax.ShapeDtypeStruct((rows, wide...]
where the time goes in v4:
time: 75.6 us; the launch traced here: 74.2 us
  Pallas kernels  66.2 us (88%)
  local copies, waits for them, and re-layouts  6.73 us (9%)
  between operations  1.32 us (2%)
    pallas_call x1, Pallas kernels, local(): pl.pallas_call(functools.partial(layer_kernel, doms), out_shape=(jax.Shap...  44.5 us
    pallas_call x1, Pallas kernels, local(): pl.pallas_call(functools.partial(build_kernel, width), out_shape=(jax.Sha...  20 us
    unnamed x16, local copies, waits for them, and re-layouts  6.73 us
    pallas_call x1, Pallas kernels, local(): pl.pallas_call(finish_kernel, out_shape=(jax.ShapeDtypeStruct((rows, wide...  1.74 us

profile of v4, /device:TPU:0, one launch (start us, length us, event | category | flops | bytes accessed | tf_op | source)
XLA Modules:
  0.0 74.2 jit_solution(5148783308146654509)
XLA Ops:
  1.3 0.0 copy-start
  1.3 1.0 %copy-done = bf16[1024,256]{1,0:T(8,128)(2,1)S(1)} copy-done((bf16[1024,256]{1,0:T(8,128)(2,1)S(1)}, bf16[1024,256]{1,0:T(8,128)(2,1)}, u32[]{:S(2)}) %copy-start) | copy-done | bytes 524312
  2.3 0.0 copy-start.4
  2.3 0.8 %copy-done.4 = s32[1,1,8192]{2,1,0:T(1,128)S(1)} copy-done((s32[1,1,8192]{2,1,0:T(1,128)S(1)}, s32[1,1,8192]{2,1,0:T(1,128)}, u32[]{:S(2)}) %copy-start.4) | copy-done | bytes 32792
  3.1 0.0 copy-start.5
  3.1 0.8 %copy-done.5 = s32[1,1,8192]{2,1,0:T(1,128)S(1)} copy-done((s32[1,1,8192]{2,1,0:T(1,128)S(1)}, s32[1,1,8192]{2,1,0:T(1,128)}, u32[]{:S(2)}) %copy-start.5) | copy-done | bytes 32792
  3.8 0.0 copy-start.6
  3.8 0.7 copy-done.6
  4.5 20.0 %count_edges.1 = (bf16[16,1088,256]{2,1,0:T(8,128)(2,1)S(1)}, f32[4,8,256]{2,1,0:T(8,128)S(1)}, f32[64,256]{1,0:T(8,128)S(1)}, s32[1,64]{1,0:T(1,128)S(1)}) custom-call(s32[1,1,8192]{2,1,0:T(1,128)S(1)} %copy-done.4, s32[1,1,8192]{2,1,0:T(1,128)S(1)} %copy-done.5, bf16[1024,256]{1,0:T(8,128)(2,1)S(1)} %copy-done, s32[1]{0:T(128)} %bitcast.1.count_ref, ...), custom_call_target="tpu_custom_call" | custom-call | tf_op jit(solution)/shard_map/count_edges/pallas_call | solution.py:484
  24.5 0.0 copy-start.1
  24.5 1.0 %copy-done.1 = bf16[1024,256]{1,0:T(8,128)(2,1)S(1)} copy-done((bf16[1024,256]{1,0:T(8,128)(2,1)S(1)}, bf16[1024,256]{1,0:T(8,128)(2,1)}, u32[]{:S(2)}) %copy-start.1) | copy-done | bytes 524312
  25.5 0.0 copy-start.2
  25.5 0.9 %copy-done.2 = bf16[256,256]{1,0:T(8,128)(2,1)S(1)} copy-done((bf16[256,256]{1,0:T(8,128)(2,1)S(1)}, bf16[256,256]{1,0:T(8,128)(2,1)}, u32[]{:S(2)}) %copy-start.2) | copy-done | bytes 131096
  26.4 0.0 copy-start.3
  26.4 0.9 %copy-done.3 = bf16[256,256]{1,0:T(8,128)(2,1)S(1)} copy-done((bf16[256,256]{1,0:T(8,128)(2,1)S(1)}, bf16[256,256]{1,0:T(8,128)(2,1)}, u32[]{:S(2)}) %copy-start.3) | copy-done | bytes 131096
  27.4 0.0 copy-start.7
  27.4 0.7 copy-done.7
  28.0 44.5 %layer.1 = (bf16[1024,256]{1,0:T(8,128)(2,1)S(1)}, f32[1024,256]{1,0:T(8,128)S(1)}, f32[64,256]{1,0:T(8,128)S(1)}) custom-call(bf16[16,1088,256]{2,1,0:T(8,128)(2,1)S(1)} %get-tuple-element.9.adjacency_ref, f32[4,8,256]{2,1,0:T(8,128)S(1)} %get-tuple-element.10.degree_ref, f32[64,256]{1,0:T(8,128)S(1)} %get-tuple-element.11.picked_ref, ...), custom_call_target="tpu_custom_call" | custom-call | tf_op jit(solution)/shard_map/layer/pallas_call | solution.py:513
  72.5 1.7 %finish.1 = (bf16[1024,256]{1,0:T(8,128)(2,1)}, f32[1024,256]{1,0:T(8,128)}) custom-call(bf16[1024,256]{1,0:T(8,128)(2,1)S(1)} %get-tuple-element.12.part_act_ref, f32[1024,256]{1,0:T(8,128)S(1)} %get-tuple-element.13.part_grad_ref, f32[64,256]{1,0:T(8,128)S(1)} %get-tuple-element.14.returned_ref, s32[1,64]{1,0:T(1,128)S(1)} %get-tuple-element.15.row_ref), custom_call_target="tpu_custom_call" | custom-call | tf_op jit(solution)/shard_map/finish/pallas_call | solution.py:555
Async XLA Ops:
  1.3 1.0 %copy-start = (bf16[1024,256]{1,0:T(8,128)(2,1)S(1)}, bf16[1024,256]{1,0:T(8,128)(2,1)}, u32[]{:S(2)}) copy-start(bf16[1024,256]{1,0:T(8,128)(2,1)} %feature_hbm.3) | copy-start | bytes 1572868
  2.3 0.8 %copy-start.4 = (s32[1,1,8192]{2,1,0:T(1,128)S(1)}, s32[1,1,8192]{2,1,0:T(1,128)}, u32[]{:S(2)}) copy-start(s32[1,1,8192]{2,1,0:T(1,128)} %source_hbm.1) | copy-start | bytes 98308
  3.1 0.8 %copy-start.5 = (s32[1,1,8192]{2,1,0:T(1,128)S(1)}, s32[1,1,8192]{2,1,0:T(1,128)}, u32[]{:S(2)}) copy-start(s32[1,1,8192]{2,1,0:T(1,128)} %target_hbm.1) | copy-start | bytes 98308
  3.8 0.7 copy-start.6
  24.5 1.0 %copy-start.1 = (bf16[1024,256]{1,0:T(8,128)(2,1)S(1)}, bf16[1024,256]{1,0:T(8,128)(2,1)}, u32[]{:S(2)}) copy-start(bf16[1024,256]{1,0:T(8,128)(2,1)} %cotangent_hbm.1) | copy-start | bytes 1572868
  25.5 0.9 %copy-start.2 = (bf16[256,256]{1,0:T(8,128)(2,1)S(1)}, bf16[256,256]{1,0:T(8,128)(2,1)}, u32[]{:S(2)}) copy-start(bf16[256,256]{1,0:T(8,128)(2,1)} %self_hbm.1) | copy-start | bytes 393220
  26.4 0.9 %copy-start.3 = (bf16[256,256]{1,0:T(8,128)(2,1)S(1)}, bf16[256,256]{1,0:T(8,128)(2,1)}, u32[]{:S(2)}) copy-start(bf16[256,256]{1,0:T(8,128)(2,1)} %neigh_hbm.1) | copy-start | bytes 393220
  27.4 0.7 copy-start.7

commit v5 on v4

--- a/solution.py
+++ b/solution.py
@@ -18,13 +18,15 @@
     return max(rows for rows in range(16, 321, 16) if width % rows == 0)
 
 
-def build_kernel(width, source_hbm, target_hbm, feature_hbm, count_ref, sender_ref,
+def build_kernel(width, source_hbm, target_hbm, feature_hbm, sender_hbm, count_ref,
                  adjacency_ref, degree_ref, picked_ref, row_ref,
-                 source_ref, target_ref, feature_ref, word_vmem, word_ref, unit, stage, in_sem, stage_sem, *tables):
+                 source_ref, target_ref, feature_ref, sender_ref, word_vmem, word_ref, keys, even, odd, stage,
+                 in_sem, stage_sem, *tables):
     incoming = [
         pltpu.make_async_copy(source_hbm.at[0], source_ref, in_sem.at[0]),
         pltpu.make_async_copy(target_hbm.at[0], target_ref, in_sem.at[1]),
         pltpu.make_async_copy(feature_hbm, feature_ref, in_sem.at[2]),
+        pltpu.make_async_copy(sender_hbm, sender_ref, in_sem.at[4]),
     ]
     for copy in incoming:
         copy.start()
@@ -38,17 +40,16 @@
 
     incoming[0].wait()
     incoming[1].wait()
+    edges = target_ref.shape[1]
     target = target_ref[...]
     within = target % accounts
-    word_vmem[...] = ((within // 128) * width + source_ref[...]) * 512 + (target // accounts) * 128 + within % 128
+    word_vmem[...] = (within // 128) * width + source_ref[...]
     word_copy = pltpu.make_async_copy(word_vmem, word_ref, in_sem.at[3])
     word_copy.start()
-
-    row_at = lax.broadcasted_iota(jnp.int32, unit.shape, 0)
-    lane_at = lax.broadcasted_iota(jnp.int32, unit.shape, 1)
-    unit[...] = sum(
-        jnp.where(row_at == lane_at + 128 * field, 1 << (8 * field), 0).astype(jnp.int32) for field in range(4)
-    )
+    key = (target // accounts) * 128 + within % 128
+    for tile in range(edges // 128):
+        keys[tile : tile + 1, :] = key[:, tile * 128 : tile * 128 + 128]
+
     zeros = jnp.zeros((128, 128), jnp.int32)
 
     def clear(chosen):
@@ -62,25 +63,33 @@
     clear(tables)
     word_copy.wait()
     incoming[2].wait()
-
-    def edge_tile(tile, carry):
-        base = tile * 128
-        for group in range(0, 128, 2 * lanes):
-            words = [word_ref[0, base + group + k] for k in range(2 * lanes)]
-            rows = [lax.shift_right_logical(word, 9) for word in words]
-            units = [word & 511 for word in words]
-            sums = []
+    incoming[3].wait()
+
+    lane_at = lax.broadcasted_iota(jnp.int32, (128, 128), 1)
+
+    def one_hot(out, tile):
+        held = jnp.minimum(tile, edges // 128 - 1)
+        key = jnp.broadcast_to(keys[pl.ds(held, 1), :], (128, 128)).T
+        amount = lax.shift_left(jnp.where(tile < tiles, 1, 0), lax.shift_right_logical(key, 7) * 8)
+        out[...] = jnp.where(lane_at == (key & 127), amount, 0)
+
+    def add_tile(rows_of, tile):
+        base = jnp.minimum(tile, edges // 128 - 1) * 128
+        for group in range(0, 128, lanes):
+            rows = [pl.ds(word_ref[0, base + group + k], 1) for k in range(lanes)]
+            sums = [tables[k][rows[k], :] + rows_of[group + k : group + k + 1, :] for k in range(lanes)]
             for k in range(lanes):
-                again = jnp.where(rows[k] == rows[k + lanes], units[k], 512)
-                first = unit[pl.ds(units[k], 1), :]
-                second = unit[pl.ds(units[k + lanes], 1), :] + unit[pl.ds(again, 1), :]
-                sums.append((tables[k][pl.ds(rows[k], 1), :] + first, tables[k][pl.ds(rows[k + lanes], 1), :] + second))
-            for k in range(lanes):
-                tables[k][pl.ds(rows[k], 1), :] = sums[k][0]
-                tables[k][pl.ds(rows[k + lanes], 1), :] = sums[k][1]
+                tables[k][rows[k], :] = sums[k]
+
+    def edge_tiles(pair, carry):
+        one_hot(odd, 2 * pair + 1)
+        add_tile(even, 2 * pair)
+        one_hot(even, 2 * pair + 2)
+        add_tile(odd, 2 * pair + 1)
         return carry
 
-    lax.fori_loop(0, tiles, edge_tile, 0)
+    one_hot(even, 0)
+    lax.fori_loop(0, (tiles + 1) // 2, edge_tiles, 0)
 
     peers, capacity = sender_ref.shape[2:]
     slots = peers * capacity
@@ -144,13 +153,17 @@
             clear(tables[:1])
 
             def one(edge, carry):
-                word = word_ref[0, edge]
-                match = jnp.where(lax.shift_right_logical(word, 7) % 4 == field, 1, 0)
-                rows = pl.ds(lax.shift_right_logical(word, 9), 1)
-                table[rows, :] = table[rows, :] + unit[pl.ds(word & 127, 1), :] * match
+                rows = pl.ds(word_ref[0, edge], 1)
+                amount = even[pl.ds(edge % 128, 1), :]
+                match = lax.shift_right_logical(amount, 8 * field) & 255
+                table[rows, :] = table[rows, :] + match
                 return carry
 
-            lax.fori_loop(0, tiles * 128, one, 0)
+            def tile_pass(tile, carry):
+                one_hot(even, tile)
+                return lax.fori_loop(tile * 128, tile * 128 + 128, one, carry)
+
+            lax.fori_loop(0, tiles, tile_pass, 0)
             for piece in range(per_block):
                 for side in range(2):
                     value = table[pl.ds((2 * piece + side) * width, width), :].astype(F32)
@@ -476,10 +489,11 @@
     chunks = rows * columns // CHUNK
     per_block = rows // CHUNK
     edges = edge_src.shape[2]
-    limit = (36 if width <= 1152 else 58) * 1024 * 1024
+    limit = 58 * 1024 * 1024
     vmem = pl.BlockSpec(memory_space=pltpu.VMEM)
     smem = pl.BlockSpec(memory_space=pltpu.SMEM)
     anywhere = pl.BlockSpec(memory_space=pl.ANY)
+    hbm = pl.BlockSpec(memory_space=pltpu.HBM)
 
     adjacency, degree, picked, row = pl.pallas_call(
         functools.partial(build_kernel, width),
@@ -489,22 +503,25 @@
             jax.ShapeDtypeStruct((slots, features_wide), F32),
             jax.ShapeDtypeStruct((1, slots), jnp.int32),
         ),
-        in_specs=[anywhere, anywhere, anywhere, smem, vmem],
+        in_specs=[hbm, hbm, hbm, hbm, smem],
         out_specs=(anywhere, vmem, vmem, vmem),
         scratch_shapes=[
             pltpu.VMEM((1, edges), jnp.int32),
             pltpu.VMEM((1, edges), jnp.int32),
             pltpu.VMEM((rows, features_wide), BF16),
+            pltpu.VMEM(send_rows.shape, jnp.int32),
             pltpu.VMEM((1, edges), jnp.int32),
             pltpu.SMEM((1, edges), jnp.int32),
-            pltpu.VMEM((520, 128), jnp.int32),
+            pltpu.VMEM((edges // 128, 128), jnp.int32),
+            pltpu.VMEM((128, 128), jnp.int32),
+            pltpu.VMEM((128, 128), jnp.int32),
             pltpu.VMEM((chunks, width, CHUNK), BF16),
-            pltpu.SemaphoreType.DMA((4,)),
+            pltpu.SemaphoreType.DMA((5,)),
             pltpu.SemaphoreType.DMA((chunks,)),
         ] + [pltpu.VMEM((rows // 128 * width, 128), jnp.int32)] * 4,
         compiler_params=pltpu.CompilerParams(vmem_limit_bytes=limit),
         name="count_edges",
-    )(edge_src, edge_dst, features, tile_count.reshape(1), send_rows)
+    )(edge_src, edge_dst, features, send_rows, tile_count.reshape(1))
 
     wide = features_wide
     dma = pltpu.SemaphoreType.DMA
@@ -517,7 +534,7 @@
             jax.ShapeDtypeStruct((rows, wide), F32),
             jax.ShapeDtypeStruct((slots, wide), F32),
         ),
-        in_specs=[anywhere] * 8,
+        in_specs=[anywhere] * 3 + [hbm] * 5,
         out_specs=(anywhere, anywhere, anywhere),
         scratch_shapes=[
             pltpu.VMEM((rows, wide), BF16),

time: 75.6 us -> 79.9 us (1.057); the launches traced: 74.2 us -> 79.7 us
  Pallas kernels: 66.2 us -> 78.4 us
  local copies, waits for them, and re-layouts: 6.73 us -> 0 us
    pallas_call x1, Pallas kernels: 1.74 us -> 17.7 us  [local(): pl.pallas_call(finish_kernel, out_shape=(jax.ShapeDtypeStruct((rows, wide...]
    pallas_call x1, Pallas kernels: 20 us -> 11.6 us  [local(): pl.pallas_call(functools.partial(build_kernel, width), out_shape=(jax.Sha...]
    unnamed x16 -> x0, local copies, waits for them, and re-layouts: 6.73 us -> none
    pallas_call x1, Pallas kernels: 44.5 us -> 49.1 us  [local(): pl.pallas_call(functools.partial(layer_kernel, doms), out_shape=(jax.Shap...]
where the time goes in v5:
time: 79.9 us; the launch traced here: 79.7 us
  Pallas kernels  78.4 us (98%)
  between operations  1.29 us (2%)
    pallas_call x1, Pallas kernels, local(): pl.pallas_call(functools.partial(layer_kernel, doms), out_shape=(jax.Shap...  49.1 us
    pallas_call x1, Pallas kernels, local(): pl.pallas_call(finish_kernel, out_shape=(jax.ShapeDtypeStruct((rows, wide...  17.7 us
    pallas_call x1, Pallas kernels, local(): pl.pallas_call(functools.partial(build_kernel, width), out_shape=(jax.Sha...  11.6 us

profile of v5, /device:TPU:0, one launch (start us, length us, event | category | flops | bytes accessed | tf_op | source)
XLA Modules:
  0.0 79.7 jit_solution(137047465371563283)
XLA Ops:
  1.3 11.6 %count_edges.1 = (bf16[16,1088,256]{2,1,0:T(8,128)(2,1)}, f32[4,8,256]{2,1,0:T(8,128)}, f32[64,256]{1,0:T(8,128)}, s32[1,64]{1,0:T(1,128)}) custom-call(s32[1,1,8192]{2,1,0:T(1,128)} %source_hbm.1, s32[1,1,8192]{2,1,0:T(1,128)} %target_hbm.1, bf16[1024,256]{1,0:T(8,128)(2,1)} %feature_hbm.3, s32[1,1,8,8]{3,2,1,0:T(8,128)} %sender_hbm.1, s32[1]{0:T(128)} %bitcast.1.count_ref), custom_call_target="tpu_custom_call" | custom-call | tf_op jit(solution)/shard_map/count_edges/pallas_call | solution.py:498
  12.9 49.1 %layer.1 = (bf16[1024,256]{1,0:T(8,128)(2,1)}, f32[1024,256]{1,0:T(8,128)}, f32[64,256]{1,0:T(8,128)}) custom-call(bf16[16,1088,256]{2,1,0:T(8,128)(2,1)} %get-tuple-element.9.adjacency_ref, f32[4,8,256]{2,1,0:T(8,128)} %get-tuple-element.10.degree_ref, f32[64,256]{1,0:T(8,128)} %get-tuple-element.11.picked_ref, bf16[1024,256]{1,0:T(8,128)(2,1)} %feature_hbm.3, ...), custom_call_target="tpu_custom_call" | custom-call | tf_op jit(solution)/shard_map/layer/pallas_call | solution.py:530
  62.0 17.7 %finish.1 = (bf16[1024,256]{1,0:T(8,128)(2,1)}, f32[1024,256]{1,0:T(8,128)}) custom-call(bf16[1024,256]{1,0:T(8,128)(2,1)} %get-tuple-element.12.part_act_ref, f32[1024,256]{1,0:T(8,128)} %get-tuple-element.13.part_grad_ref, f32[64,256]{1,0:T(8,128)} %get-tuple-element.14.returned_ref, s32[1,64]{1,0:T(1,128)} %get-tuple-element.15.row_ref), custom_call_target="tpu_custom_call" | custom-call | tf_op jit(solution)/shard_map/finish/pallas_call | solution.py:572

commit v6 on v5

--- a/solution.py
+++ b/solution.py
@@ -226,49 +226,49 @@
     incoming[0].start()
     load_block(diagonal)
     load_block(opposite)
+    pl.semaphore_wait(barrier, 3 + doms - 1)
+
+    def slot(at):
+        return pl.ds(pl.multiple_of(at * capacity, capacity), capacity)
+
+    def halo_copy(step):
+        peer = lax.rem(part + step, doms)
+        return pltpu.make_async_remote_copy(
+            src_ref=picked_ref.at[slot(peer)], dst_ref=halo.at[slot(part)],
+            send_sem=halo_send.at[step], recv_sem=halo_recv.at[step],
+            device_id=(peer, source), device_id_type=MESH)
+
+    def back_copy(step):
+        peer = lax.rem(part + step, doms)
+        return pltpu.make_async_remote_copy(
+            src_ref=halo_grad.at[slot(peer)], dst_ref=returned.at[slot(part)],
+            send_sem=back_send.at[step], recv_sem=back_recv.at[step],
+            device_id=(peer, source), device_id_type=MESH)
+
+    def each_peer(action):
+        def go(step, carry):
+            action(step)
+            return carry
+
+        lax.fori_loop(1, doms, go, 0)
+
+    each_peer(lambda step: halo_copy(step).start())
+
+    def degree_copy(step):
+        peer = lax.rem(source + step, 4)
+        return pltpu.make_async_remote_copy(
+            src_ref=degree_ref.at[peer], dst_ref=degree_in.at[step],
+            send_sem=degree_send.at[step], recv_sem=degree_recv.at[step],
+            device_id=(part, peer), device_id_type=MESH)
+
+    for step in range(1, 4):
+        degree_copy(step).start()
     for copy in incoming[1:]:
         copy.start()
     load_block(sibling)
     load_block(source)
     incoming[0].wait()
     table_t[...] = feature_ref[...].astype(F32).T.astype(BF16)
-    pl.semaphore_wait(barrier, 3 + doms - 1)
-
-    def slot(at):
-        return pl.ds(pl.multiple_of(at * capacity, capacity), capacity)
-
-    def halo_copy(step):
-        peer = lax.rem(part + step, doms)
-        return pltpu.make_async_remote_copy(
-            src_ref=picked_ref.at[slot(peer)], dst_ref=halo.at[slot(part)],
-            send_sem=halo_send.at[step], recv_sem=halo_recv.at[step],
-            device_id=(peer, source), device_id_type=MESH)
-
-    def back_copy(step):
-        peer = lax.rem(part + step, doms)
-        return pltpu.make_async_remote_copy(
-            src_ref=halo_grad.at[slot(peer)], dst_ref=returned.at[slot(part)],
-            send_sem=back_send.at[step], recv_sem=back_recv.at[step],
-            device_id=(peer, source), device_id_type=MESH)
-
-    def each_peer(action):
-        def go(step, carry):
-            action(step)
-            return carry
-
-        lax.fori_loop(1, doms, go, 0)
-
-    each_peer(lambda step: halo_copy(step).start())
-
-    def degree_copy(step):
-        peer = lax.rem(source + step, 4)
-        return pltpu.make_async_remote_copy(
-            src_ref=degree_ref.at[peer], dst_ref=degree_in.at[step],
-            send_sem=degree_send.at[step], recv_sem=degree_recv.at[step],
-            device_id=(part, peer), device_id_type=MESH)
-
-    for step in range(1, 4):
-        degree_copy(step).start()
 
     def part_copy(kind, step):
         source_ref, target_ref, peer = (
@@ -312,8 +312,9 @@
         load(at).wait()
         kept[step] = from_local(at)
 
-    each_chunk(early)
-    each_chunk(early_kept)
+    for step in range(2):
+        early(step)
+        early_kept(step)
     halo[slot(part), :] = jnp.zeros((capacity, halo.shape[1]), F32)
     returned[slot(part), :] = jnp.zeros((capacity, halo.shape[1]), F32)
     each_peer(lambda step: halo_copy(step).wait_recv())
@@ -323,7 +324,11 @@
         to_sibling[step] = (foreign[step] + from_halo(diagonal * per_block + step)).astype(BF16)
         part_copy(0, step).start()
 
-    each_chunk(send_foreign)
+    send_foreign(0)
+    send_foreign(1)
+    for step in range(2, per_block):
+        early(step)
+        send_foreign(step)
 
     def send_chip(step):
         mine = kept[step] + from_halo(opposite * per_block + step)
@@ -333,6 +338,8 @@
 
     send_chip(0)
     send_chip(1)
+    for step in range(2, per_block):
+        early_kept(step)
 
     def send_own(step):
         at = sibling * per_block + step
@@ -451,13 +458,14 @@
     returned_out.wait()
 
 
-def finish_kernel(part_act_ref, part_grad_ref, returned_ref, row_ref, act_ref, grad_ref, grad, returned, sem):
+def finish_kernel(part_act_ref, part_grad_ref, returned_ref, row_ref, act_ref, grad_ref, act, grad, returned, sem):
     pieces = grad_ref.shape[0] // CHUNK
 
     def piece(at):
         return pl.ds(at * CHUNK, CHUNK)
 
-    act = pltpu.make_async_copy(part_act_ref, act_ref, sem.at[0])
+    act_in = pltpu.make_async_copy(part_act_ref, act, sem.at[0])
+    act_out = pltpu.make_async_copy(act, act_ref, sem.at[0])
     back = pltpu.make_async_copy(returned_ref, returned, sem.at[1])
     come = [
         pltpu.make_async_copy(part_grad_ref.at[piece(at)], grad.at[piece(at)], sem.at[2 + at]) for at in range(pieces)
@@ -465,7 +473,7 @@
     back.start()
     for copy in come:
         copy.start()
-    act.start()
+    act_in.start()
     back.wait()
     rows = returned[...].astype(BF16)
     leave = []
@@ -476,7 +484,9 @@
         grad[piece(at), :] += added
         leave.append(pltpu.make_async_copy(grad.at[piece(at)], grad_ref.at[piece(at)], sem.at[2 + pieces + at]))
         leave[-1].start()
-    act.wait()
+    act_in.wait()
+    act_out.start()
+    act_out.wait()
     for copy in leave:
         copy.wait()
 
@@ -577,7 +587,12 @@
         ),
         in_specs=[anywhere, anywhere, anywhere, vmem],
         out_specs=(anywhere, anywhere),
-        scratch_shapes=[pltpu.VMEM((rows, wide), F32), pltpu.VMEM((slots, wide), F32), dma((2 + 2 * per_block,))],
+        scratch_shapes=[
+            pltpu.VMEM((rows, wide), BF16),
+            pltpu.VMEM((rows, wide), F32),
+            pltpu.VMEM((slots, wide), F32),
+            dma((2 + 2 * per_block,)),
+        ],
         compiler_params=pltpu.CompilerParams(vmem_limit_bytes=limit),
         name="finish",
     )(part_act, part_grad, returned, row)

time: 79.9 us -> 65.8 us (0.82)
  Pallas kernels: 78.4 us -> 64.3 us
    pallas_call x1, Pallas kernels: 17.7 us -> 3.2 us  [local(): pl.pallas_call(finish_kernel, out_shape=(jax.ShapeDtypeStruct((rows, wide...]
    pallas_call x1, Pallas kernels: 11.6 us -> 13.6 us  [local(): pl.pallas_call(functools.partial(build_kernel, width), out_shape=(jax.Sha...]
    pallas_call x1, Pallas kernels: 49.1 us -> 47.5 us  [local(): pl.pallas_call(functools.partial(layer_kernel, doms), out_shape=(jax.Shap...]
where the time goes in v6:
time: 65.8 us; the launch traced here: 65.6 us
  Pallas kernels  64.3 us (98%)
  between operations  1.29 us (2%)
    pallas_call x1, Pallas kernels, local(): pl.pallas_call(functools.partial(layer_kernel, doms), out_shape=(jax.Shap...  47.5 us
    pallas_call x1, Pallas kernels, local(): pl.pallas_call(functools.partial(build_kernel, width), out_shape=(jax.Sha...  13.6 us
    pallas_call x1, Pallas kernels, local(): pl.pallas_call(finish_kernel, out_shape=(jax.ShapeDtypeStruct((rows, wide...  3.2 us

profile of v6, /device:TPU:0, one launch (start us, length us, event | category | flops | bytes accessed | tf_op | source)
XLA Modules:
  0.0 65.6 jit_solution(2872244724678412552)
XLA Ops:
  1.3 13.6 %count_edges.1 = (bf16[16,1088,256]{2,1,0:T(8,128)(2,1)}, f32[4,8,256]{2,1,0:T(8,128)}, f32[64,256]{1,0:T(8,128)}, s32[1,64]{1,0:T(1,128)}) custom-call(s32[1,1,8192]{2,1,0:T(1,128)} %source_hbm.1, s32[1,1,8192]{2,1,0:T(1,128)} %target_hbm.1, bf16[1024,256]{1,0:T(8,128)(2,1)} %feature_hbm.3, s32[1,1,8,8]{3,2,1,0:T(8,128)} %sender_hbm.1, s32[1]{0:T(128)} %bitcast.1.count_ref), custom_call_target="tpu_custom_call" | custom-call | tf_op jit(solution)/shard_map/count_edges/pallas_call | solution.py:508
  14.9 47.5 %layer.1 = (bf16[1024,256]{1,0:T(8,128)(2,1)}, f32[1024,256]{1,0:T(8,128)}, f32[64,256]{1,0:T(8,128)}) custom-call(bf16[16,1088,256]{2,1,0:T(8,128)(2,1)} %get-tuple-element.9.adjacency_ref, f32[4,8,256]{2,1,0:T(8,128)} %get-tuple-element.10.degree_ref, f32[64,256]{1,0:T(8,128)} %get-tuple-element.11.picked_ref, bf16[1024,256]{1,0:T(8,128)(2,1)} %feature_hbm.3, ...), custom_call_target="tpu_custom_call" | custom-call | tf_op jit(solution)/shard_map/layer/pallas_call | solution.py:540
  62.4 3.2 %finish.1 = (bf16[1024,256]{1,0:T(8,128)(2,1)}, f32[1024,256]{1,0:T(8,128)}) custom-call(bf16[1024,256]{1,0:T(8,128)(2,1)} %get-tuple-element.12.part_act_ref, f32[1024,256]{1,0:T(8,128)} %get-tuple-element.13.part_grad_ref, f32[64,256]{1,0:T(8,128)} %get-tuple-element.14.returned_ref, s32[1,64]{1,0:T(1,128)} %get-tuple-element.15.row_ref), custom_call_target="tpu_custom_call" | custom-call | tf_op jit(solution)/shard_map/finish/pallas_call | solution.py:582
